TPU v7x, 128 devices: a whole 4x4x4 slice. The times are simulated.
128 devices in a mesh: section: 8 (over y, x_hi), dp: 16 (over z, x_lo, core).
Axes of the slice: x: 4 (x_hi: 2, x_lo: 2; x = x_hi * 2 + x_lo), y: 4, z: 4, core: 2. Of those that a mesh axis runs over, the one named last changes fastest.
Arguments:
- inputs: bfloat16 [16, 2, 1, 128, 1024], P('dp'), may hold values from -120 to 120
- cotangent: bfloat16 [16, 2, 1, 128, 1024], P('dp'), may hold values from -0.4375 to 0.4375
- w_qkv: bfloat16 [8, 1024, 1536], P('section'), may hold values from -0.1875 to 0.1875
- w_out: bfloat16 [8, 1024, 1024], P('section'), may hold values from -0.1875 to 0.1875
Outputs:
- grad_qkv: float32 [8, 1024, 1536], P('section', 'dp')
- grad_out: float32 [8, 1024, 1024], P('section', 'dp')
All inputs are finite; a program needn't handle non-finite values.
Results may differ from a plain program's by a relative error of at most 0.039.
Values may be sent and summed in bfloat16 or wider, within the bound.
A program may use at most 128 MiB of HBM per device.

v0:
```python
import jax
import jax.numpy as jnp
from jax import lax
from jax.sharding import PartitionSpec as P

HD = 64
QH = 16
KH = 4


EPSILON = 1e-05


def swapped(block, axis, apart):
    count = lax.axis_size(axis)
    route = []
    for low in range(count):
        high = low | 1 << apart
        if high != low and high < count:
            route += [(low, high), (high, low)]
    return lax.ppermute(block, axis, route)


def from_behind(array, axis, by):
    size = lax.axis_size(axis)
    pairs = [(i, i + by) for i in range(size) if 0 <= i + by < size]
    return lax.ppermute(array, axis, pairs)


def split_heads(joined):
    leading = joined.shape[:2]
    q_width = QH * HD
    kv_width = KH * HD
    queries = joined[..., :q_width].reshape(leading + (KH, QH // KH, HD))
    key_heads = joined[..., q_width : q_width + kv_width].reshape(leading + (KH, HD))
    value_heads = joined[..., q_width + kv_width :].reshape(leading + (KH, HD))
    return (queries, key_heads, value_heads)


def layer_forward(hidden, pair_qkv, pair_out):
    leading = hidden.shape[:2]
    seq_len = hidden.shape[1]
    widened = hidden.astype(jnp.float32)
    inverse = lax.rsqrt(jnp.mean(widened * widened, axis=-1, keepdims=True) + EPSILON)
    normed = (widened * inverse).astype(jnp.bfloat16)
    joined = jnp.einsum(
        "ptd,pdo->pto", normed, pair_qkv, preferred_element_type=jnp.float32
    ).astype(jnp.bfloat16)
    queries, key_heads, value_heads = split_heads(joined)
    scores = jnp.einsum(
        "pikgd,pjkd->pkgij", queries, key_heads, preferred_element_type=jnp.float32
    ) * HD ** (-0.5)
    causal = jnp.tril(jnp.ones((seq_len, seq_len), dtype=jnp.bool_))
    exponent = jnp.where(causal, jnp.exp(scores), 0.0)
    attn_probs = (exponent / jnp.sum(exponent, axis=-1, keepdims=True)).astype(jnp.bfloat16)
    mixture = jnp.einsum(
        "pkgij,pjkd->pikgd", attn_probs, value_heads, preferred_element_type=jnp.float32
    )
    attention = mixture.reshape(leading + (QH * HD,)).astype(jnp.bfloat16)
    update = jnp.einsum("ptq,pdq->ptd", attention, pair_out, preferred_element_type=jnp.float32)
    result = (widened + update).astype(jnp.bfloat16)
    return (result, (hidden, normed, joined, attn_probs, attention))


def layer_backward(cotangents, hidden, joined, attn_probs, pair_qkv, pair_out, full_pass):
    leading = joined.shape[:2]
    queries, key_heads, value_heads = split_heads(joined)
    d_attention = jnp.einsum(
        "ptd,pdq->ptq", cotangents, pair_out, preferred_element_type=jnp.float32
    ).astype(jnp.bfloat16)
    d_heads = d_attention.reshape(leading + (KH, QH // KH, HD))
    d_probs = jnp.einsum(
        "pikgd,pjkd->pkgij", d_heads, value_heads, preferred_element_type=jnp.float32
    )
    d_values = jnp.einsum(
        "pkgij,pikgd->pjkd", attn_probs, d_heads, preferred_element_type=jnp.float32
    )
    probs_wide = attn_probs.astype(jnp.float32)
    d_scores = (
        probs_wide
        * (d_probs - jnp.sum(probs_wide * d_probs, axis=-1, keepdims=True))
        * HD ** (-0.5)
    ).astype(jnp.bfloat16)
    d_queries = jnp.einsum(
        "pkgij,pjkd->pikgd", d_scores, key_heads, preferred_element_type=jnp.float32
    )
    d_keys = jnp.einsum("pkgij,pikgd->pjkd", d_scores, queries, preferred_element_type=jnp.float32)
    d_joined = jnp.concatenate(
        [
            d_queries.reshape(leading + (QH * HD,)),
            d_keys.reshape(leading + (KH * HD,)),
            d_values.reshape(leading + (KH * HD,)),
        ],
        axis=-1,
    ).astype(jnp.bfloat16)
    if not full_pass:
        return (None, d_joined)
    d_normed = jnp.einsum("pto,pdo->ptd", d_joined, pair_qkv, preferred_element_type=jnp.float32)
    widened = hidden.astype(jnp.float32)
    inverse = lax.rsqrt(jnp.mean(widened * widened, axis=-1, keepdims=True) + EPSILON)
    scaled = widened * inverse
    d_hidden = (
        cotangents.astype(jnp.float32)
        + inverse * (d_normed - scaled * jnp.mean(d_normed * scaled, axis=-1, keepdims=True))
    ).astype(jnp.bfloat16)
    return (d_hidden, d_joined)


def entering(source_grouped, tick_number, offsets, entry_here, received):
    micro_count = source_grouped.shape[1]
    relative = tick_number - offsets
    is_valid = jnp.logical_and(relative >= 0, relative < micro_count)
    clamped = jnp.clip(relative, 0, micro_count - 1)
    picked = jnp.stack(
        [
            lax.dynamic_index_in_dim(source_grouped[0], clamped[0], 0, keepdims=False),
            lax.dynamic_index_in_dim(source_grouped[1], clamped[1], 0, keepdims=False),
        ]
    )
    chosen = jnp.logical_and(is_valid, entry_here)
    return jnp.where(chosen[:, None, None], picked, received)


def by_micro(stacked, offsets, micro_count):
    pieces = []
    for pipe_index in range(2):
        anchor = (offsets[pipe_index], pipe_index) + (0,) * (stacked.ndim - 2)
        extent = (micro_count, 1) + stacked.shape[2:]
        pieces.append(lax.dynamic_slice(stacked, anchor, extent)[:, 0])
    return jnp.stack(pieces)


def at_micro(grouped, indices):
    pieces = []
    for pipe_index in range(2):
        anchor = (pipe_index, indices[pipe_index]) + (0,) * (grouped.ndim - 2)
        extent = (1, 1) + grouped.shape[2:]
        pieces.append(lax.dynamic_slice(grouped, anchor, extent)[0, 0])
    return jnp.stack(pieces)


def on_device(inputs, cotangent, w_qkv, w_out):
    sections = lax.axis_size("section")
    replicas = lax.axis_size("dp")
    position = lax.axis_index("section")
    replica_rank = lax.axis_index("dp")
    mirror_position = sections - 1 - position
    own_qkv = w_qkv[0]
    own_out = w_out[0]
    model_width = own_qkv.shape[0]
    qkv_width = own_qkv.shape[1]
    slice_rows = model_width // replicas
    travelling = jnp.concatenate(
        [
            lax.dynamic_slice_in_dim(own_qkv, replica_rank * slice_rows, slice_rows, 0),
            lax.dynamic_slice_in_dim(own_out, replica_rank * slice_rows, slice_rows, 0),
        ],
        axis=1,
    )
    for bit_number in range(sections.bit_length() - 1):
        travelling = swapped(travelling, "section", bit_number)
    mirror_joined = lax.all_gather(travelling, "dp", axis=0, tiled=True)
    pair_qkv = jnp.stack([own_qkv, mirror_joined[:, :qkv_width]])
    pair_out = jnp.stack([own_out, mirror_joined[:, qkv_width:]])
    entries = inputs[0]
    targets = cotangent[0]
    micro_count = entries.shape[1]
    tick_count = micro_count + sections - 1
    forward_offsets = jnp.stack([position, mirror_position])
    forward_entry = jnp.stack([position == 0, position == sections - 1])
    backward_offsets = jnp.stack([mirror_position, position])
    backward_entry = jnp.stack([position == sections - 1, position == 0])
    start_rows = jnp.zeros((2,) + entries.shape[2:], jnp.bfloat16)

    def forward_tick(received, tick_number):
        current = entering(entries, tick_number, forward_offsets, forward_entry, received)
        result, retained = layer_forward(current, pair_qkv, pair_out)
        down_next = from_behind(result[0], "section", 1)
        up_next = from_behind(result[1], "section", -1)
        return (jnp.stack([down_next, up_next]), retained)

    received, retained_stack = lax.scan(forward_tick, start_rows, jnp.arange(tick_count - 1))
    final_input = entering(entries, tick_count - 1, forward_offsets, forward_entry, received)
    unused_result, retained_last = layer_forward(final_input, pair_qkv, pair_out)
    per_micro = tuple(
        (
            by_micro(
                jnp.concatenate([stacked_part, last_part[None]], axis=0),
                forward_offsets,
                micro_count,
            )
            for stacked_part, last_part in zip(retained_stack, retained_last)
        )
    )
    stored_hidden, stored_normed, stored_joined, stored_probs, stored_attention = per_micro

    def backward_tick(received, tick_number):
        incoming = entering(targets, tick_number, backward_offsets, backward_entry, received)
        indices = jnp.clip(tick_number - backward_offsets, 0, micro_count - 1)
        d_hidden, d_joined = layer_backward(
            incoming,
            at_micro(stored_hidden, indices),
            at_micro(stored_joined, indices),
            at_micro(stored_probs, indices),
            pair_qkv,
            pair_out,
            True,
        )
        down_back = from_behind(d_hidden[0], "section", -1)
        up_back = from_behind(d_hidden[1], "section", 1)
        return (jnp.stack([down_back, up_back]), (incoming, d_joined))

    received_back, grad_stack = lax.scan(backward_tick, start_rows, jnp.arange(tick_count - 1))
    last_incoming = entering(
        targets, tick_count - 1, backward_offsets, backward_entry, received_back
    )
    last_indices = jnp.clip(tick_count - 1 - backward_offsets, 0, micro_count - 1)
    unused_hidden, last_joined = layer_backward(
        last_incoming,
        at_micro(stored_hidden, last_indices),
        at_micro(stored_joined, last_indices),
        at_micro(stored_probs, last_indices),
        pair_qkv,
        pair_out,
        False,
    )
    incoming_all = by_micro(
        jnp.concatenate([grad_stack[0], last_incoming[None]], axis=0), backward_offsets, micro_count
    )
    joined_all = by_micro(
        jnp.concatenate([grad_stack[1], last_joined[None]], axis=0), backward_offsets, micro_count
    )
    normed_rows = stored_normed.reshape(2, -1, model_width)
    attn_rows = stored_attention.reshape(2, -1, stored_attention.shape[-1])
    upstream_rows = incoming_all.reshape(2, -1, model_width)
    joined_rows = joined_all.reshape(2, -1, qkv_width)
    part_qkv = jnp.einsum(
        "prc,pro->cpo", normed_rows, joined_rows, preferred_element_type=jnp.float32
    )
    part_out = jnp.einsum(
        "prc,prq->cpq", upstream_rows, attn_rows, preferred_element_type=jnp.float32
    )
    summed = lax.psum_scatter(
        jnp.concatenate([part_qkv, part_out], axis=2).astype(jnp.bfloat16),
        "dp",
        scatter_dimension=0,
        tiled=True,
    ).astype(jnp.float32)
    partner = summed[:, 1]
    for bit_number in range(sections.bit_length() - 1):
        partner = swapped(partner.astype(jnp.bfloat16), "section", bit_number).astype(partner.dtype)
    combined = summed[:, 0] + partner
    return (combined[:, :qkv_width][None], combined[:, qkv_width:][None])


def solution(mesh):
    placed = (
        P("dp", None, None, None, None),
        P("dp", None, None, None, None),
        P("section", None, None),
        P("section", None, None),
    )
    return jax.shard_map(
        on_device,
        mesh=mesh,
        in_specs=placed,
        out_specs=(P("section", "dp", None), P("section", "dp", None)),
        check_vma=False,
    )
```

profile of v0, /device:TPU:0, one launch (start us, length us, event | category | flops | bytes accessed | tf_op | source)
XLA Modules:
  0.0 922.1 jit_solution(16032660431400079508)
XLA Ops:
  12.4 7.7 collective-permute-done.4
  21.9 6.8 collective-permute-done.5
  32.1 6.3 collective-permute-done.6
  42.7 38.0 %all-gather.2.cloned.1.call-done = bf16[1024,2560]{1,0:T(8,128)(2,1)} async-done(((bf16[64,2560]{1,0:T(8,128)(2,1)}), bf16[1024,2560]{1,0:T(8,128)(2,1)}) %all-gather.2.cloned.1.call-update) | async-done | bytes 5242896 | tf_op jit(solution)/shard_map/all_gather | solution.py:162
  94.3 179.0 %while.38 = (s32[]{:T(128)}, bf16[2,128,1024]{2,1,0:T(8,128)(2,1)S(1)}, bf16[7,2,128,1024]{3,2,1,0:T(8,128)(2,1)}, bf16[7,2,128,1024]{3,2,0,1:T(8,128)(2,1)}, bf...) while((s32[]{:T(128)}, ...), condition=%wide.region_3.4_spmd, body=%wide.region_0.3_spmd.sunk | while | flops 1484402944 | bytes 51729704 | solution.py:182
  108.3 6.1 collective-permute-start.1
  134.1 6.5 collective-permute-start.1
  159.8 7.4 collective-permute-start.1
  185.6 7.4 collective-permute-start.1
  211.0 7.4 collective-permute-start.1
  236.3 7.6 collective-permute-start.1
  261.9 7.4 collective-permute-start.1
  290.3 299.9 %while.39 = (s32[]{:T(128)}, bf16[2,128,1024]{2,1,0:T(8,128)(2,1)S(1)}, bf16[7,2,128,1024]{3,2,0,1:T(8,128)(2,1)}, bf16[7,2,128,1536]{2,3,0,1:T(8,128)(2,1)}, s3...) while((s32[]{:T(128)}, ...), condition=%wide.region_10.11_spmd, body=%wide.region_6.10_spmd.sunk | while | flops 1627791872 | bytes 41166084 | solution.py:213
  316.7 7.0 collective-permute-start.2
  327.5 8.8 collective-permute-done.3
  362.6 6.0 collective-permute-start.2
  372.5 7.3 collective-permute-done.3
  406.1 5.5 collective-permute-start.2
  415.5 7.4 collective-permute-done.3
  449.2 6.6 collective-permute-start.2
  459.7 7.3 collective-permute-done.3
  493.3 6.0 collective-permute-start.2
  503.2 7.3 collective-permute-done.3
  543.5 6.9 collective-permute-done.3
  583.2 7.0 collective-permute-done.3
  601.4 5.8 maximum_maximum_fusion
  615.4 10.8 %pad_maximum_fusion.2 = bf16[1024,2,2560]{0,2,1:T(8,128)(2,1)} fusion(bf16[1024,2,1024]{0,2,1:T(8,128)(2,1)S(1)} %convert_bitcast_fusion.1, bf16[1024,2,1536]{0,2,1:T(8,128)(2,1)S(1)} %convert_bitcast_fusion), kind=kLoop, calls=%fused_computation.74 | loop fusion | flops 20971520 | bytes 20971520 | tf_op jit(solution)/shard_map/concatenate | solution.py:244
  626.2 26.6 %copy.141 = bf16[1024,2,2560]{2,1,0:T(2,128)(2,1)} copy(bf16[1024,2,2560]{0,2,1:T(8,128)(2,1)} %pad_maximum_fusion.2) | data formatting | bytes 20971520 | tf_op jit(solution)/shard_map/concatenate | solution.py:244
  654.7 231.1 %all-reduce.3.cloned.1.call-done = bf16[1024,2,2560]{2,1,0:T(2,128)(2,1)} async-done(((bf16[1024,2,2560]{2,1,0:T(2,128)(2,1)}), bf16[1024,2,2560]{2,1,0:T(2,128)(2,1)}) %all-reduce.3.cloned.1.call-update) | async-done | bytes 10485776
  890.9 6.5 collective-permute-done.7
  898.9 5.6 collective-permute-done.8
  908.3 5.5 collective-permute-done.9
  (475 shorter events, 421.5 us)
Async XLA Ops:
  7.2 73.5 %all-gather.2.cloned.1.call-start = ((), (), s32[]{:S(2)}) async-start(), calls=%async_computation | async-start | bytes 5570560 | tf_op jit(solution)/shard_map/all_gather | solution.py:162
  9.2 10.9 %collective-permute-start.4 = (bf16[64,2560]{1,0:T(8,128)(2,1)S(1)}, bf16[64,2560]{1,0:T(8,128)(2,1)S(1)}, u32[]{:S(2)}, u32[]{:S(2)}) collective-permute-start(bf16[64,2560]{1,0:T(8,128)(2,1)S(1)} %pad_maximum_fusion.10), channel_id=1, source_target_pairs={{0,16},{16,0},{32,48},{48,32},{64,80},{80,64},{96,112},{112,96},{1... | collective-permute-start | bytes 983048 | tf_op jit(solution)/shard_map/ppermute | solution.py:21
  28.7 9.6 %collective-permute-start.6 = (bf16[64,2560]{1,0:T(8,128)(2,1)S(1)}, bf16[64,2560]{1,0:T(8,128)(2,1)S(1)}, u32[]{:S(2)}, u32[]{:S(2)}) collective-permute-start(bf16[64,2560]{1,0:T(8,128)(2,1)S(1)} %collective-permute-done.5), channel_id=1, source_target_pairs={{0,64},{64,0},{16,80},{80,16},{32,96},{96,32},{48,112},{112,48},{1... | collective-permute-start | bytes 983048 | tf_op jit(solution)/shard_map/ppermute | solution.py:21
  39.1 846.7 %all-reduce.3.cloned.1.call-start = ((), (), s32[]{:S(2)}) async-start(), calls=%async_computation.1 | async-start | bytes 20971520
  107.0 12.1 %collective-permute-start = (bf16[128,1024]{1,0:T(8,128)(2,1)S(1)}, bf16[128,1024]{1,0:T(8,128)(2,1)S(1)}, u32[]{:S(2)}, u32[]{:S(2)}) collective-permute-start(bf16[128,1024]{1,0:T(8,128)(2,1)S(1)} %get-tuple-element.658), channel_id=1, source_target_pairs={{16,0},{32,16},{48,32},{64,48},{80,64},{96,80},{112,96},{17,1},{33... | collective-permute-start | bytes 786440 | tf_op jit(solution)/shard_map/while/body/eval_jaxpr/ppermute | solution.py:27
  108.3 11.7 %collective-permute-start.1 = (bf16[128,1024]{1,0:T(8,128)(2,1)S(1)}, bf16[128,1024]{1,0:T(8,128)(2,1)S(1)}, u32[]{:S(2)}, u32[]{:S(2)}) collective-permute-start(bf16[128,1024]{1,0:T(8,128)(2,1)S(1)} %get-tuple-element.659), channel_id=1, source_target_pairs={{0,16},{16,32},{32,48},{48,64},{64,80},{80,96},{96,112},{1,17},{17... | collective-permute-start | bytes 786440 | tf_op jit(solution)/shard_map/while/body/eval_jaxpr/ppermute | solution.py:27
  132.8 11.8 %collective-permute-start = (bf16[128,1024]{1,0:T(8,128)(2,1)S(1)}, bf16[128,1024]{1,0:T(8,128)(2,1)S(1)}, u32[]{:S(2)}, u32[]{:S(2)}) collective-permute-start(bf16[128,1024]{1,0:T(8,128)(2,1)S(1)} %get-tuple-element.658), channel_id=1, source_target_pairs={{16,0},{32,16},{48,32},{64,48},{80,64},{96,80},{112,96},{17,1},{33... | collective-permute-start | bytes 786440 | tf_op jit(solution)/shard_map/while/body/eval_jaxpr/ppermute | solution.py:27
  134.1 11.6 %collective-permute-start.1 = (bf16[128,1024]{1,0:T(8,128)(2,1)S(1)}, bf16[128,1024]{1,0:T(8,128)(2,1)S(1)}, u32[]{:S(2)}, u32[]{:S(2)}) collective-permute-start(bf16[128,1024]{1,0:T(8,128)(2,1)S(1)} %get-tuple-element.659), channel_id=1, source_target_pairs={{0,16},{16,32},{32,48},{48,64},{64,80},{80,96},{96,112},{1,17},{17... | collective-permute-start | bytes 786440 | tf_op jit(solution)/shard_map/while/body/eval_jaxpr/ppermute | solution.py:27
  158.5 11.7 %collective-permute-start = (bf16[128,1024]{1,0:T(8,128)(2,1)S(1)}, bf16[128,1024]{1,0:T(8,128)(2,1)S(1)}, u32[]{:S(2)}, u32[]{:S(2)}) collective-permute-start(bf16[128,1024]{1,0:T(8,128)(2,1)S(1)} %get-tuple-element.658), channel_id=1, source_target_pairs={{16,0},{32,16},{48,32},{64,48},{80,64},{96,80},{112,96},{17,1},{33... | collective-permute-start | bytes 786440 | tf_op jit(solution)/shard_map/while/body/eval_jaxpr/ppermute | solution.py:27
  159.8 11.6 %collective-permute-start.1 = (bf16[128,1024]{1,0:T(8,128)(2,1)S(1)}, bf16[128,1024]{1,0:T(8,128)(2,1)S(1)}, u32[]{:S(2)}, u32[]{:S(2)}) collective-permute-start(bf16[128,1024]{1,0:T(8,128)(2,1)S(1)} %get-tuple-element.659), channel_id=1, source_target_pairs={{0,16},{16,32},{32,48},{48,64},{64,80},{80,96},{96,112},{1,17},{17... | collective-permute-start | bytes 786440 | tf_op jit(solution)/shard_map/while/body/eval_jaxpr/ppermute | solution.py:27
  184.3 11.1 %collective-permute-start = (bf16[128,1024]{1,0:T(8,128)(2,1)S(1)}, bf16[128,1024]{1,0:T(8,128)(2,1)S(1)}, u32[]{:S(2)}, u32[]{:S(2)}) collective-permute-start(bf16[128,1024]{1,0:T(8,128)(2,1)S(1)} %get-tuple-element.658), channel_id=1, source_target_pairs={{16,0},{32,16},{48,32},{64,48},{80,64},{96,80},{112,96},{17,1},{33... | collective-permute-start | bytes 786440 | tf_op jit(solution)/shard_map/while/body/eval_jaxpr/ppermute | solution.py:27
  185.6 11.3 %collective-permute-start.1 = (bf16[128,1024]{1,0:T(8,128)(2,1)S(1)}, bf16[128,1024]{1,0:T(8,128)(2,1)S(1)}, u32[]{:S(2)}, u32[]{:S(2)}) collective-permute-start(bf16[128,1024]{1,0:T(8,128)(2,1)S(1)} %get-tuple-element.659), channel_id=1, source_target_pairs={{0,16},{16,32},{32,48},{48,64},{64,80},{80,96},{96,112},{1,17},{17... | collective-permute-start | bytes 786440 | tf_op jit(solution)/shard_map/while/body/eval_jaxpr/ppermute | solution.py:27
  209.7 11.6 %collective-permute-start = (bf16[128,1024]{1,0:T(8,128)(2,1)S(1)}, bf16[128,1024]{1,0:T(8,128)(2,1)S(1)}, u32[]{:S(2)}, u32[]{:S(2)}) collective-permute-start(bf16[128,1024]{1,0:T(8,128)(2,1)S(1)} %get-tuple-element.658), channel_id=1, source_target_pairs={{16,0},{32,16},{48,32},{64,48},{80,64},{96,80},{112,96},{17,1},{33... | collective-permute-start | bytes 786440 | tf_op jit(solution)/shard_map/while/body/eval_jaxpr/ppermute | solution.py:27
  211.0 11.3 %collective-permute-start.1 = (bf16[128,1024]{1,0:T(8,128)(2,1)S(1)}, bf16[128,1024]{1,0:T(8,128)(2,1)S(1)}, u32[]{:S(2)}, u32[]{:S(2)}) collective-permute-start(bf16[128,1024]{1,0:T(8,128)(2,1)S(1)} %get-tuple-element.659), channel_id=1, source_target_pairs={{0,16},{16,32},{32,48},{48,64},{64,80},{80,96},{96,112},{1,17},{17... | collective-permute-start | bytes 786440 | tf_op jit(solution)/shard_map/while/body/eval_jaxpr/ppermute | solution.py:27
  235.0 12.2 %collective-permute-start = (bf16[128,1024]{1,0:T(8,128)(2,1)S(1)}, bf16[128,1024]{1,0:T(8,128)(2,1)S(1)}, u32[]{:S(2)}, u32[]{:S(2)}) collective-permute-start(bf16[128,1024]{1,0:T(8,128)(2,1)S(1)} %get-tuple-element.658), channel_id=1, source_target_pairs={{16,0},{32,16},{48,32},{64,48},{80,64},{96,80},{112,96},{17,1},{33... | collective-permute-start | bytes 786440 | tf_op jit(solution)/shard_map/while/body/eval_jaxpr/ppermute | solution.py:27
  236.3 11.5 %collective-permute-start.1 = (bf16[128,1024]{1,0:T(8,128)(2,1)S(1)}, bf16[128,1024]{1,0:T(8,128)(2,1)S(1)}, u32[]{:S(2)}, u32[]{:S(2)}) collective-permute-start(bf16[128,1024]{1,0:T(8,128)(2,1)S(1)} %get-tuple-element.659), channel_id=1, source_target_pairs={{0,16},{16,32},{32,48},{48,64},{64,80},{80,96},{96,112},{1,17},{17... | collective-permute-start | bytes 786440 | tf_op jit(solution)/shard_map/while/body/eval_jaxpr/ppermute | solution.py:27
  260.6 12.1 %collective-permute-start = (bf16[128,1024]{1,0:T(8,128)(2,1)S(1)}, bf16[128,1024]{1,0:T(8,128)(2,1)S(1)}, u32[]{:S(2)}, u32[]{:S(2)}) collective-permute-start(bf16[128,1024]{1,0:T(8,128)(2,1)S(1)} %get-tuple-element.658), channel_id=1, source_target_pairs={{16,0},{32,16},{48,32},{64,48},{80,64},{96,80},{112,96},{17,1},{33... | collective-permute-start | bytes 786440 | tf_op jit(solution)/shard_map/while/body/eval_jaxpr/ppermute | solution.py:27
  261.9 11.3 %collective-permute-start.1 = (bf16[128,1024]{1,0:T(8,128)(2,1)S(1)}, bf16[128,1024]{1,0:T(8,128)(2,1)S(1)}, u32[]{:S(2)}, u32[]{:S(2)}) collective-permute-start(bf16[128,1024]{1,0:T(8,128)(2,1)S(1)} %get-tuple-element.659), channel_id=1, source_target_pairs={{0,16},{16,32},{32,48},{48,64},{64,80},{80,96},{96,112},{1,17},{17... | collective-permute-start | bytes 786440 | tf_op jit(solution)/shard_map/while/body/eval_jaxpr/ppermute | solution.py:27
  316.7 10.8 %collective-permute-start.2 = (bf16[128,1024]{1,0:T(8,128)(2,1)S(1)}, bf16[128,1024]{1,0:T(8,128)(2,1)S(1)}, u32[]{:S(2)}, u32[]{:S(2)}) collective-permute-start(bf16[128,1024]{1,0:T(8,128)(2,1)S(1)} %get-tuple-element.681), channel_id=1, source_target_pairs={{0,16},{16,32},{32,48},{48,64},{64,80},{80,96},{96,112},{1,17},{17... | collective-permute-start | bytes 786440 | tf_op jit(solution)/shard_map/while/body/eval_jaxpr/ppermute | solution.py:27
  323.7 12.6 %collective-permute-start.3 = (bf16[128,1024]{1,0:T(8,128)(2,1)S(1)}, bf16[128,1024]{1,0:T(8,128)(2,1)S(1)}, u32[]{:S(2)}, u32[]{:S(2)}) collective-permute-start(bf16[128,1024]{1,0:T(8,128)(2,1)S(1)} %get-tuple-element.682), channel_id=1, source_target_pairs={{16,0},{32,16},{48,32},{64,48},{80,64},{96,80},{112,96},{17,1},{33... | collective-permute-start | bytes 786440 | tf_op jit(solution)/shard_map/while/body/eval_jaxpr/ppermute | solution.py:27
  362.6 9.9 %collective-permute-start.2 = (bf16[128,1024]{1,0:T(8,128)(2,1)S(1)}, bf16[128,1024]{1,0:T(8,128)(2,1)S(1)}, u32[]{:S(2)}, u32[]{:S(2)}) collective-permute-start(bf16[128,1024]{1,0:T(8,128)(2,1)S(1)} %get-tuple-element.681), channel_id=1, source_target_pairs={{0,16},{16,32},{32,48},{48,64},{64,80},{80,96},{96,112},{1,17},{17... | collective-permute-start | bytes 786440 | tf_op jit(solution)/shard_map/while/body/eval_jaxpr/ppermute | solution.py:27
  368.6 11.1 %collective-permute-start.3 = (bf16[128,1024]{1,0:T(8,128)(2,1)S(1)}, bf16[128,1024]{1,0:T(8,128)(2,1)S(1)}, u32[]{:S(2)}, u32[]{:S(2)}) collective-permute-start(bf16[128,1024]{1,0:T(8,128)(2,1)S(1)} %get-tuple-element.682), channel_id=1, source_target_pairs={{16,0},{32,16},{48,32},{64,48},{80,64},{96,80},{112,96},{17,1},{33... | collective-permute-start | bytes 786440 | tf_op jit(solution)/shard_map/while/body/eval_jaxpr/ppermute | solution.py:27
  406.1 9.4 %collective-permute-start.2 = (bf16[128,1024]{1,0:T(8,128)(2,1)S(1)}, bf16[128,1024]{1,0:T(8,128)(2,1)S(1)}, u32[]{:S(2)}, u32[]{:S(2)}) collective-permute-start(bf16[128,1024]{1,0:T(8,128)(2,1)S(1)} %get-tuple-element.681), channel_id=1, source_target_pairs={{0,16},{16,32},{32,48},{48,64},{64,80},{80,96},{96,112},{1,17},{17... | collective-permute-start | bytes 786440 | tf_op jit(solution)/shard_map/while/body/eval_jaxpr/ppermute | solution.py:27
  411.6 11.3 %collective-permute-start.3 = (bf16[128,1024]{1,0:T(8,128)(2,1)S(1)}, bf16[128,1024]{1,0:T(8,128)(2,1)S(1)}, u32[]{:S(2)}, u32[]{:S(2)}) collective-permute-start(bf16[128,1024]{1,0:T(8,128)(2,1)S(1)} %get-tuple-element.682), channel_id=1, source_target_pairs={{16,0},{32,16},{48,32},{64,48},{80,64},{96,80},{112,96},{17,1},{33... | collective-permute-start | bytes 786440 | tf_op jit(solution)/shard_map/while/body/eval_jaxpr/ppermute | solution.py:27
  449.2 10.5 %collective-permute-start.2 = (bf16[128,1024]{1,0:T(8,128)(2,1)S(1)}, bf16[128,1024]{1,0:T(8,128)(2,1)S(1)}, u32[]{:S(2)}, u32[]{:S(2)}) collective-permute-start(bf16[128,1024]{1,0:T(8,128)(2,1)S(1)} %get-tuple-element.681), channel_id=1, source_target_pairs={{0,16},{16,32},{32,48},{48,64},{64,80},{80,96},{96,112},{1,17},{17... | collective-permute-start | bytes 786440 | tf_op jit(solution)/shard_map/while/body/eval_jaxpr/ppermute | solution.py:27
  455.8 11.2 %collective-permute-start.3 = (bf16[128,1024]{1,0:T(8,128)(2,1)S(1)}, bf16[128,1024]{1,0:T(8,128)(2,1)S(1)}, u32[]{:S(2)}, u32[]{:S(2)}) collective-permute-start(bf16[128,1024]{1,0:T(8,128)(2,1)S(1)} %get-tuple-element.682), channel_id=1, source_target_pairs={{16,0},{32,16},{48,32},{64,48},{80,64},{96,80},{112,96},{17,1},{33... | collective-permute-start | bytes 786440 | tf_op jit(solution)/shard_map/while/body/eval_jaxpr/ppermute | solution.py:27
  493.3 9.9 %collective-permute-start.2 = (bf16[128,1024]{1,0:T(8,128)(2,1)S(1)}, bf16[128,1024]{1,0:T(8,128)(2,1)S(1)}, u32[]{:S(2)}, u32[]{:S(2)}) collective-permute-start(bf16[128,1024]{1,0:T(8,128)(2,1)S(1)} %get-tuple-element.681), channel_id=1, source_target_pairs={{0,16},{16,32},{32,48},{48,64},{64,80},{80,96},{96,112},{1,17},{17... | collective-permute-start | bytes 786440 | tf_op jit(solution)/shard_map/while/body/eval_jaxpr/ppermute | solution.py:27
  499.3 11.2 %collective-permute-start.3 = (bf16[128,1024]{1,0:T(8,128)(2,1)S(1)}, bf16[128,1024]{1,0:T(8,128)(2,1)S(1)}, u32[]{:S(2)}, u32[]{:S(2)}) collective-permute-start(bf16[128,1024]{1,0:T(8,128)(2,1)S(1)} %get-tuple-element.682), channel_id=1, source_target_pairs={{16,0},{32,16},{48,32},{64,48},{80,64},{96,80},{112,96},{17,1},{33... | collective-permute-start | bytes 786440 | tf_op jit(solution)/shard_map/while/body/eval_jaxpr/ppermute | solution.py:27
  539.6 10.8 %collective-permute-start.3 = (bf16[128,1024]{1,0:T(8,128)(2,1)S(1)}, bf16[128,1024]{1,0:T(8,128)(2,1)S(1)}, u32[]{:S(2)}, u32[]{:S(2)}) collective-permute-start(bf16[128,1024]{1,0:T(8,128)(2,1)S(1)} %get-tuple-element.682), channel_id=1, source_target_pairs={{16,0},{32,16},{48,32},{64,48},{80,64},{96,80},{112,96},{17,1},{33... | collective-permute-start | bytes 786440 | tf_op jit(solution)/shard_map/while/body/eval_jaxpr/ppermute | solution.py:27
  579.3 10.8 %collective-permute-start.3 = (bf16[128,1024]{1,0:T(8,128)(2,1)S(1)}, bf16[128,1024]{1,0:T(8,128)(2,1)S(1)}, u32[]{:S(2)}, u32[]{:S(2)}) collective-permute-start(bf16[128,1024]{1,0:T(8,128)(2,1)S(1)} %get-tuple-element.682), channel_id=1, source_target_pairs={{16,0},{32,16},{48,32},{64,48},{80,64},{96,80},{112,96},{17,1},{33... | collective-permute-start | bytes 786440 | tf_op jit(solution)/shard_map/while/body/eval_jaxpr/ppermute | solution.py:27
  888.2 9.3 %collective-permute-start.7 = (bf16[64,2560]{1,0:T(8,128)(2,1)S(1)}, bf16[64,2560]{1,0:T(8,128)(2,1)S(1)}, u32[]{:S(2)}, u32[]{:S(2)}) collective-permute-start(bf16[64,2560]{1,0:T(8,128)(2,1)S(1)} %bitcast.444), channel_id=1, source_target_pairs={{0,16},{16,0},{32,48},{48,32},{64,80},{80,64},{96,112},{112,96},{1... | collective-permute-start | bytes 983048 | tf_op jit(solution)/shard_map/ppermute | solution.py:21
  904.5 9.2 collective-permute-start.9
  (38 other events, 187.4 us)
Sparse Core Ops, SparseCore 0:
  39.2 41.4 all-gather.1
  652.9 232.8 all-reduce.2
where the time goes:
time: 929 us; the launch traced here: 922 us
  waiting for transfers between devices  389 us (42%)
  matrix products  186 us (20%)
  starting transfers between devices  121 us (13%)
  local copies, waits for them, and re-layouts  109 us (12%)
  other arithmetic  101 us (11%)
  between operations  15.3 us (2%)
    unnamed x3, waiting for transfers between devices  231 us
    ppermute x28, starting transfers between devices, from_behind(): return lax.ppermute(array, axis, pairs)  105 us
    ppermute x28, waiting for transfers between devices, from_behind(): return lax.ppermute(array, axis, pairs)  81 us
    dynamic_update_slice x35, other arithmetic, on_device(): lax.scan(forward_tick, start_rows, jnp.arange(tick_count - 1))  47.1 us
    ppermute x6, waiting for transfers between devices, swapped(): return lax.ppermute(block, axis, route)  38.4 us
    all_gather x1, waiting for transfers between devices, on_device(): mirror_joined = lax.all_gather(travelling, 'dp', axis=0, tiled=True)  38 us
    dot_general x8, matrix products, layer_forward(): jnp.einsum('ptd,pdo->pto', normed, pair_qkv, preferred_element_type=jnp.f...  37.3 us
    dot_general x7, matrix products, layer_backward(): jnp.einsum('pto,pdo->ptd', d_joined, pair_qkv, preferred_element_type=jnp...  36.4 us
  transfers between devices with their start and end apart: 36, of which 36 were waited for; matrix products, arithmetic and copies ran while one was open for 2% of the time, Pallas kernels for 0%

commit v1 on v0

v1 whole, which is shorter than its diff:
```python
import functools

import jax
import jax.numpy as jnp
from jax import lax
from jax.experimental import pallas as pl
from jax.experimental.pallas import tpu as pltpu
from jax.sharding import PartitionSpec as P

MESH = pl.DeviceIdType.MESH
F32 = jnp.float32
BF16 = jnp.bfloat16
EPSILON = 1e-05

D = 1024
SEQ = 128
QKV = 1536
COLS = 2560
HALF = 1280
QUARTER = 640
CHUNK = 64


def mm(a, b):
    return jnp.dot(a, b, preferred_element_type=F32)


def mm_nt(a, b):
    return lax.dot_general(a, b, (((1,), (1,)), ((), ())), preferred_element_type=F32)


def mm_tn(a, b):
    return lax.dot_general(a, b, (((0,), (0,)), ((), ())), preferred_element_type=F32)


def block_diagonal(pair, group):
    low = lax.broadcasted_iota(jnp.int32, pair.shape, 1) < 64
    wide = pair.astype(F32)
    rolled = pltpu.roll(wide, 64, 1)
    first, second = (wide, rolled) if group % 2 == 0 else (rolled, wide)
    zero = jnp.zeros_like(wide)
    return jnp.concatenate([jnp.where(low, first, zero), jnp.where(low, zero, second)], axis=0).astype(BF16)


def half_sums(x):
    return (jnp.sum(x[:, :128], axis=1, keepdims=True), jnp.sum(x[:, 128:], axis=1, keepdims=True))


def stack_pairs(x, group):
    at = group * 256
    return jnp.concatenate([x[:, at : at + 128], x[:, at + 128 : at + 256]], axis=0)


def kv_pairs(joined, group):
    at = (group // 2) * 128
    return joined[:, D + at : D + at + 128], joined[:, D + 256 + at : D + 256 + at + 128]


def attention_forward(joined, probs_ref, att_ref, layer):
    rows = lax.broadcasted_iota(jnp.int32, (256, 256), 0) & 127
    cols = lax.broadcasted_iota(jnp.int32, (256, 256), 1) & 127
    causal = rows >= cols
    for group in range(4):
        queries = stack_pairs(joined, group)
        keys, values = kv_pairs(joined, group)
        scores = mm_nt(queries, block_diagonal(keys, group)) * 0.125
        exponent = jnp.where(causal, jnp.exp(scores), 0.0)
        left, right = half_sums(exponent)
        probs = jnp.concatenate([exponent[:, :128] / left, exponent[:, 128:] / right], axis=1).astype(BF16)
        probs_ref[layer, group] = probs
        mixed = mm(probs, block_diagonal(values, group)).astype(BF16)
        at = group * 256
        att_ref[layer, 0:SEQ, at : at + 128] = mixed[:128]
        att_ref[layer, 0:SEQ, at + 128 : at + 256] = mixed[128:]


def attention_backward(joined, d_attention, probs_ref, dj_ref, layer):
    d_keys, d_values = [], []
    for group in range(4):
        queries = stack_pairs(joined, group)
        d_heads = stack_pairs(d_attention, group)
        keys, values = kv_pairs(joined, group)
        probs = probs_ref[layer, group]
        d_probs = mm_nt(d_heads, block_diagonal(values, group))
        wide = probs.astype(F32)
        left, right = half_sums(wide * d_probs)
        centred = jnp.concatenate([d_probs[:, :128] - left, d_probs[:, 128:] - right], axis=1)
        d_scores = (wide * centred * 0.125).astype(BF16)
        d_queries = mm(d_scores, block_diagonal(keys, group)).astype(BF16)
        at = group * 256
        dj_ref[layer, 0:SEQ, at : at + 128] = d_queries[:128]
        dj_ref[layer, 0:SEQ, at + 128 : at + 256] = d_queries[128:]
        d_keys.append(mm_tn(d_scores, queries))
        d_values.append(mm_tn(probs, d_heads))
    low = lax.broadcasted_iota(jnp.int32, (128, 128), 1) < 64

    def merged(even, odd):
        first = even[:128] + pltpu.roll(even[128:], 64, 1)
        second = pltpu.roll(odd[:128], 64, 1) + odd[128:]
        return jnp.where(low, first, second).astype(BF16)

    for pair in range(2):
        at = D + pair * 128
        dj_ref[layer, 0:SEQ, at : at + 128] = merged(d_keys[2 * pair], d_keys[2 * pair + 1])
        dj_ref[layer, 0:SEQ, at + 256 : at + 384] = merged(d_values[2 * pair], d_values[2 * pair + 1])


def inverse_norm(wide):
    return lax.rsqrt(jnp.mean(wide * wide, axis=-1, keepdims=True) + EPSILON)


def kernel(
    inputs_ref, cotangent_ref, wq_ref, wo_ref,
    gq_ref, go_ref,
    wq, wo, hidden, normed, joined, probs, att, upstream, dj, grads,
    z_a1, z_b1, z_m2, z_p2, z_r, z_sa1, z_sb1, z_sm2, z_sp2,
    x_a1, x_b1, x_m2, x_p2, x_r, x_sa1, x_sb1, x_sm2, x_sp2,
    load_sem, flip_send, flip_recv, spread_send, spread_recv, core_send, core_recv,
    hop_send, hop_recv, share_send, share_recv, sum_send, sum_recv,
):
    section, dp = lax.axis_index("section"), lax.axis_index("dp")
    y, x_hi = lax.div(section, 2), lax.rem(section, 2)
    z, x_lo, core = lax.div(dp, 4), lax.rem(lax.div(dp, 2), 2), lax.rem(dp, 2)
    x = 2 * x_hi + x_lo

    def place(y, x, z, core):
        return (2 * y + lax.div(x, 2), 4 * z + 2 * lax.rem(x, 2) + core)

    core_dev = place(y, x, z, 1 - core)
    xp_dev, xm_dev = place(y, lax.rem(x + 1, 4), z, core), place(y, lax.rem(x + 3, 4), z, core)
    zp_dev, zm_dev = place(y, x, lax.rem(z + 1, 4), core), place(y, x, lax.rem(z + 3, 4), core)
    yp_dev, ym_dev = place(lax.rem(y + 1, 4), x, z, core), place(lax.rem(y + 3, 4), x, z, core)
    flip_dev = place(y, 3 - x, z, core)
    side_dev = place(y, 2 * x_hi + 1 - x_lo, z, core)

    def remote(src, dst, send_sem, recv_sem, device):
        return pltpu.make_async_remote_copy(
            src_ref=src, dst_ref=dst, send_sem=send_sem, recv_sem=recv_sem, device_id=device, device_id_type=MESH
        )

    sent = []

    def go(copy):
        copy.start()
        sent.append(copy)

    loads = [
        pltpu.make_async_copy(wq_ref.at[0], wq.at[x_hi], load_sem.at[0]),
        pltpu.make_async_copy(wo_ref.at[0], wo.at[x_hi], load_sem.at[1]),
    ]
    load_in = pltpu.make_async_copy(inputs_ref.at[0, x_hi, 0], hidden.at[0], load_sem.at[2])
    load_cot = pltpu.make_async_copy(cotangent_ref.at[0, x_hi, 0], upstream.at[2, 0:SEQ], load_sem.at[3])
    for copy in loads:
        copy.start()

    @pl.when(y == 0)
    def _():
        load_in.start()

    @pl.when(y == 3)
    def _():
        load_cot.start()

    barrier = pltpu.get_barrier_semaphore()
    for device in (core_dev, xp_dev, xm_dev, zp_dev, zm_dev, yp_dev, ym_dev):
        pl.semaphore_signal(barrier, inc=1, device_id=device, device_id_type=MESH)
    pl.semaphore_wait(barrier, 7)

    other = 1 - x_hi
    piece = lax.rem(z + 2 * x_lo, 4)
    pieces = [lax.rem(piece + k, 4) for k in range(4)]

    def chunk_rows(which, half, part):
        return pl.ds(pl.multiple_of(which * 256 + half * 128 + (part % 2) * CHUNK, CHUNK), CHUNK)

    def chunk(buf_q, buf_o, slot, which, half, part):
        rows = chunk_rows(which, half, part)
        return (buf_q if part < 2 else buf_o).at[slot, rows]

    for part in range(4):
        src = chunk(wq_ref, wo_ref, 0, pieces[2], core, part)
        go(remote(src, chunk(wq, wo, x_hi, pieces[2], core, part), flip_send.at[part], flip_recv.at[part], flip_dev))

    def await_flip(part):
        block = chunk(wq, wo, other, pieces[0], core, part)
        remote(block, block, flip_send.at[part], flip_recv.at[part], flip_dev).wait_recv()

    def spread(part):
        block = chunk(wq, wo, other, pieces[0], core, part)
        for slot, device in ((1, zm_dev), (2, side_dev), (3, zp_dev)):
            go(remote(block, block, spread_send.at[part, slot], spread_recv.at[part, slot], device))

    def to_core(part, k):
        block = chunk(wq, wo, other, pieces[k], core, part)
        go(remote(block, block, core_send.at[part, k], core_recv.at[part, k], core_dev))

    def gather_rest(part):
        for k in (1, 2, 3):
            block = chunk(wq, wo, other, pieces[k], core, part)
            remote(block, block, spread_send.at[part, k], spread_recv.at[part, k], side_dev).wait_recv()
            to_core(part, k)

    for part in range(4):
        await_flip(part)
        spread(part)
        to_core(part, 0)
        if part > 0:
            gather_rest(part - 1)
    gather_rest(3)
    for part in range(4):
        for k in range(4):
            block = chunk(wq, wo, other, pieces[k], 1 - core, part)
            remote(block, block, core_send.at[part, k], core_recv.at[part, k], core_dev).wait_recv()
    for copy in loads:
        copy.wait()

    h_hop = remote(hidden.at[2], hidden.at[0], hop_send.at[0], hop_recv.at[0], yp_dev)
    c_hop = remote(upstream.at[0, 0:SEQ], upstream.at[2, 0:SEQ], hop_send.at[1], hop_recv.at[1], ym_dev)

    @pl.when(y == 0)
    def _():
        load_in.wait()

    @pl.when(y > 0)
    def _():
        h_hop.wait_recv()

    def forward(layer, carry):
        h = hidden[layer]
        wide = h.astype(F32)
        inverse = inverse_norm(wide)
        normed[layer, 0:SEQ] = (wide * inverse).astype(BF16)
        joined[layer] = (mm(h, wq[layer]) * inverse).astype(BF16)
        attention_forward(joined[layer], probs, att, layer)
        hidden[layer + 1] = (wide + mm_nt(att[layer, 0:SEQ], wo[layer])).astype(BF16)
        return carry

    lax.fori_loop(0, 2, forward, 0)

    @pl.when(y < 3)
    def _():
        h_hop.start()

    def share(buf, slot, number):
        go(remote(buf.at[slot, 0:SEQ], buf.at[slot, SEQ : 2 * SEQ], share_send.at[number], share_recv.at[number], core_dev))

    shared = [(normed, 0), (normed, 1), (att, 0), (att, 1), (upstream, 2), (upstream, 1), (dj, 1), (dj, 0)]
    for number in range(4):
        share(*shared[number], number)

    @pl.when(y == 3)
    def _():
        load_cot.wait()

    @pl.when(y < 3)
    def _():
        c_hop.wait_recv()

    def backward(step, carry):
        layer = 1 - step
        c = upstream[layer + 1, 0:SEQ]
        d_attention = mm(c, wo[layer]).astype(BF16)
        attention_backward(joined[layer], d_attention, probs, dj, layer)
        d_normed = mm_nt(dj[layer, 0:SEQ], wq[layer])
        wide = hidden[layer].astype(F32)
        inverse = inverse_norm(wide)
        scaled = wide * inverse
        along = jnp.mean(d_normed * scaled, axis=-1, keepdims=True)
        upstream[layer, 0:SEQ] = (c.astype(F32) + inverse * (d_normed - scaled * along)).astype(BF16)
        return carry

    lax.fori_loop(0, 2, backward, 0)

    @pl.when(y > 0)
    def _():
        c_hop.start()

    for number in range(4, 8):
        share(*shared[number], number)
    for number, (buf, slot) in enumerate(shared):
        remote(
            buf.at[slot, 0:SEQ], buf.at[slot, SEQ : 2 * SEQ], share_send.at[number], share_recv.at[number], core_dev
        ).wait_recv()

    low = lax.broadcasted_iota(jnp.int32, (2 * SEQ, 128), 1) < 64

    def own_columns(block):
        def tile(k):
            return block[:, 128 * k : 128 * k + 128].astype(F32)

        tiles = []
        for lo in range(2):
            for pair in range(2):
                a, b = tile(4 * pair + lo), tile(4 * pair + 2 + lo)
                first = jnp.where(core == 0, a, pltpu.roll(a, 64, 1))
                second = jnp.where(core == 0, pltpu.roll(b, 64, 1), b)
                tiles.append(jnp.where(low, first, second).astype(BF16))
        return jnp.concatenate(tiles, axis=1)

    for layer in (1, 0):
        left = own_columns(normed[layer])
        for lo in range(2):
            part = mm_tn(left[:, 256 * lo : 256 * lo + 256], dj[layer]).astype(BF16)
            grads[2 * layer + lo, :, :, 0:QKV] = part.reshape(4, 64, QKV)
        left = own_columns(upstream[layer + 1])
        for lo in range(2):
            part = mm_tn(left[:, 256 * lo : 256 * lo + 256], att[layer]).astype(BF16)
            grads[2 * layer + lo, :, :, QKV:COLS] = part.reshape(4, 64, D)

    def ring_sum(view, position, plus, minus, bufs, sems):
        a1, b1, m2, p2, alpha, beta = bufs
        opposite, after, before = (lax.rem(position + k, 4) for k in (2, 1, 3))
        s, r = sum_send.at, sum_recv.at

        def first():
            go(remote(view(opposite, 0), a1, s[sems], r[sems], plus))
            go(remote(view(opposite, 1), b1, s[sems + 1], r[sems + 1], minus))
            go(remote(view(after, 1), m2.at[beta], s[sems + 2], r[sems + 2], plus))
            go(remote(view(before, 0), p2.at[alpha], s[sems + 3], r[sems + 3], minus))

        def second():
            mine = view(after, 0)
            remote(mine, a1, s[sems], r[sems], plus).wait_recv()
            mine[...] = (mine[...].astype(F32) + a1[...].astype(F32)).astype(BF16)
            go(remote(mine, m2.at[alpha], s[sems + 4], r[sems + 4], plus))
            mine = view(before, 1)
            remote(mine, b1, s[sems + 1], r[sems + 1], minus).wait_recv()
            mine[...] = (mine[...].astype(F32) + b1[...].astype(F32)).astype(BF16)
            go(remote(mine, p2.at[beta], s[sems + 5], r[sems + 5], minus))

        def last():
            remote(view(after, 1), m2.at[beta], s[sems + 2], r[sems + 2], plus).wait_recv()
            remote(view(before, 0), p2.at[alpha], s[sems + 3], r[sems + 3], minus).wait_recv()
            remote(view(after, 0), m2.at[alpha], s[sems + 4], r[sems + 4], plus).wait_recv()
            remote(view(before, 1), p2.at[beta], s[sems + 5], r[sems + 5], minus).wait_recv()

        return first, second, last

    def halves(offset):
        return [pl.ds(offset, QUARTER), pl.ds(offset + QUARTER, QUARTER)]

    z_cols, x_cols, own_cols = halves(0), halves(HALF), halves(0)
    wide_at = [(slice(None), slice(None), cols) for cols in own_cols]
    flat_at = [(slice(None), cols) for cols in own_cols]
    z_big = ring_sum(
        lambda t, k: grads.at[:, t, :, z_cols[k]], z, zp_dev, zm_dev, (z_a1, z_b1, z_m2, z_p2, *wide_at), 0
    )
    x_big = ring_sum(
        lambda t, k: grads.at[t, :, :, x_cols[k]], x, xp_dev, xm_dev, (x_a1, x_b1, x_m2, x_p2, *wide_at), 6
    )
    z_small = ring_sum(
        lambda t, k: z_r.at[t, :, own_cols[k]], x, xp_dev, xm_dev, (z_sa1, z_sb1, z_sm2, z_sp2, *flat_at), 12
    )
    x_small = ring_sum(
        lambda t, k: x_r.at[t, :, own_cols[k]], z, zp_dev, zm_dev, (x_sa1, x_sb1, x_sm2, x_sp2, *flat_at), 18
    )
    z_big[0]()
    x_big[0]()
    z_big[1]()
    x_big[1]()
    z_big[2]()
    z_r[...] = (grads[:, z, :, 0:HALF].astype(F32) + z_m2[...].astype(F32) + z_p2[...].astype(F32)).astype(BF16)
    z_small[0]()
    x_big[2]()
    x_r[...] = (grads[x, :, :, HALF:COLS].astype(F32) + x_m2[...].astype(F32) + x_p2[...].astype(F32)).astype(BF16)
    x_small[0]()
    z_small[1]()
    x_small[1]()
    z_small[2]()
    gq_ref[0, :, 0:HALF] = z_r[x].astype(F32) + z_sm2[...].astype(F32) + z_sp2[...].astype(F32)
    x_small[2]()
    total = x_r[z].astype(F32) + x_sm2[...].astype(F32) + x_sp2[...].astype(F32)
    gq_ref[0, :, HALF:QKV] = total[:, : QKV - HALF]
    go_ref[0] = total[:, QKV - HALF :]

    for copy in sent:
        copy.wait_send()

    @pl.when(y < 3)
    def _():
        h_hop.wait_send()

    @pl.when(y > 0)
    def _():
        c_hop.wait_send()


def on_device(inputs, cotangent, w_qkv, w_out):
    any_space = pl.BlockSpec(memory_space=pl.ANY)
    vmem = pl.BlockSpec(memory_space=pltpu.VMEM)
    dma = pltpu.SemaphoreType.DMA

    def flow():
        return [
            pltpu.VMEM((4, 64, QUARTER), BF16),
            pltpu.VMEM((4, 64, QUARTER), BF16),
            pltpu.VMEM((4, 64, HALF), BF16),
            pltpu.VMEM((4, 64, HALF), BF16),
            pltpu.VMEM((4, 64, HALF), BF16),
            pltpu.VMEM((64, QUARTER), BF16),
            pltpu.VMEM((64, QUARTER), BF16),
            pltpu.VMEM((64, HALF), BF16),
            pltpu.VMEM((64, HALF), BF16),
        ]

    return pl.pallas_call(
        kernel,
        out_shape=(jax.ShapeDtypeStruct((1, 64, QKV), F32), jax.ShapeDtypeStruct((1, 64, D), F32)),
        in_specs=[any_space] * 4,
        out_specs=(vmem, vmem),
        scratch_shapes=[
            pltpu.VMEM((2, D, QKV), BF16),
            pltpu.VMEM((2, D, D), BF16),
            pltpu.VMEM((3, SEQ, D), BF16),
            pltpu.VMEM((2, 2 * SEQ, D), BF16),
            pltpu.VMEM((2, SEQ, QKV), BF16),
            pltpu.VMEM((2, 4, 256, 256), BF16),
            pltpu.VMEM((2, 2 * SEQ, D), BF16),
            pltpu.VMEM((3, 2 * SEQ, D), BF16),
            pltpu.VMEM((2, 2 * SEQ, QKV), BF16),
            pltpu.VMEM((4, 4, 64, COLS), BF16),
            *flow(),
            *flow(),
            dma((4,)),
            dma((4,)),
            dma((4,)),
            dma((4, 4)),
            dma((4, 4)),
            dma((4, 4)),
            dma((4, 4)),
            dma((2,)),
            dma((2,)),
            dma((8,)),
            dma((8,)),
            dma((24,)),
            dma((24,)),
        ],
        compiler_params=pltpu.CompilerParams(
            collective_id=0, has_side_effects=True, vmem_limit_bytes=56 * 2**20
        ),
    )(inputs, cotangent, w_qkv, w_out)


def solution(mesh):
    placed = (
        P("dp", None, None, None, None),
        P("dp", None, None, None, None),
        P("section", None, None),
        P("section", None, None),
    )
    return jax.shard_map(
        on_device,
        mesh=mesh,
        in_specs=placed,
        out_specs=(P("section", "dp", None), P("section", "dp", None)),
        check_vma=False,
    )
```

time: 929 us -> 151 us (0.16)
  waiting for transfers between devices: 389 us -> 0 us
  matrix products: 186 us -> 0 us
  Pallas kernels: 0 us -> 145 us
  starting transfers between devices: 121 us -> 0 us
  local copies, waits for them, and re-layouts: 109 us -> 3.44 us
  other arithmetic: 101 us -> 0 us
  between operations: 15.3 us -> 0.64 us
    unnamed x3 -> x0, waiting for transfers between devices: 231 us -> none
    dot_general x80 -> x0, matrix products: 186 us -> none  [the longest x8 37.3 us: layer_forward(): jnp.einsum('ptd,pdo->pto', normed, pair_qkv, preferred_element_type=jnp.f...]
    pallas_call x0 -> x1, Pallas kernels: none -> 145 us  [on_device(): pl.pallas_call(kernel, out_shape=(jax.ShapeDtypeStruct((1, 64, QKV), F32)...]
    ppermute x34 -> x0, starting transfers between devices: 121 us -> none  [the longest x28 105 us: from_behind(): return lax.ppermute(array, axis, pairs)]
    ppermute x34 -> x0, waiting for transfers between devices: 119 us -> none  [the longest x28 81 us: from_behind(): return lax.ppermute(array, axis, pairs)]
    dynamic_update_slice x35 -> x0, other arithmetic: 47.1 us -> none  [on_device(): lax.scan(forward_tick, start_rows, jnp.arange(tick_count - 1))]
    all_gather x1 -> x0, waiting for transfers between devices: 38 us -> none  [on_device(): mirror_joined = lax.all_gather(travelling, 'dp', axis=0, tiled=True)]
    concatenate x1 -> x0, local copies, waits for them, and re-layouts: 26.6 us -> none  [on_device(): jnp.concatenate([part_qkv, part_out], axis=2).astype(jnp.bfloat16)]
  transfers between devices with their start and end apart: 36 -> 0, of which waited for: 36 -> 0; matrix products, arithmetic and copies ran while one was open for 2% -> 0% of each run, Pallas kernels for 0% -> 0%
where the time goes in v1:
time: 151 us; the launch traced here: 149 us
  Pallas kernels  145 us (96%)
  local copies, waits for them, and re-layouts  3.44 us (2%)
    pallas_call x1, Pallas kernels, on_device(): pl.pallas_call(kernel, out_shape=(jax.ShapeDtypeStruct((1, 64, QKV), F32)...  145 us
    unnamed x2, local copies, waits for them, and re-layouts  3.44 us

profile of v1, /device:TPU:0, one launch (start us, length us, event | category | flops | bytes accessed | tf_op | source)
XLA Modules:
  0.0 149.3 jit_solution(8898580008861488921)
XLA Ops:
  0.6 145.2 %shard_map.59 = (f32[1,64,1536]{2,1,0:T(8,128)}, f32[1,64,1024]{2,1,0:T(8,128)}) custom-call(bf16[1,2,1,128,1024]{4,3,2,1,0:T(8,128)(2,1)} %inputs_ref.1, bf16[1,2,1,128,1024]{4,3,2,1,0:T(8,128)(2,1)} %cotangent_ref.1, bf16[1,1024,1536]{2,1,0:T(8,128)(2,1)} %wq_ref.1, bf16[1,1024,1024]{2,1,0:T(8,128)(2,1)} %wo_ref.1), custom_call_target="tpu_custom_call" | custom-call | tf_op jit(solution)/shard_map/pallas_call | solution.py:406
  145.9 1.8 %copy.8 = f32[1,64,1536]{2,1,0:T(8,128)} copy(f32[1,64,1536]{2,1,0:T(8,128)} %get-tuple-element.4) | data formatting | bytes 786432
  147.6 1.7 %copy.9 = f32[1,64,1024]{2,1,0:T(8,128)} copy(f32[1,64,1024]{2,1,0:T(8,128)} %get-tuple-element.5) | data formatting | bytes 524288

commit v2 on v1

--- a/solution.py
+++ b/solution.py
@@ -112,11 +112,11 @@
 def kernel(
     inputs_ref, cotangent_ref, wq_ref, wo_ref,
     gq_ref, go_ref,
-    wq, wo, hidden, normed, joined, probs, att, upstream, dj, grads,
+    wq, wo, entry, passed, hidden, normed, joined, probs, att, upstream, dj, grads,
     z_a1, z_b1, z_m2, z_p2, z_r, z_sa1, z_sb1, z_sm2, z_sp2,
     x_a1, x_b1, x_m2, x_p2, x_r, x_sa1, x_sb1, x_sm2, x_sp2,
     load_sem, flip_send, flip_recv, spread_send, spread_recv, core_send, core_recv,
-    hop_send, hop_recv, share_send, share_recv, sum_send, sum_recv,
+    entry_send, entry_recv, hop_send, hop_recv, share_send, share_recv, sum_send, sum_recv,
 ):
     section, dp = lax.axis_index("section"), lax.axis_index("dp")
     y, x_hi = lax.div(section, 2), lax.rem(section, 2)
@@ -132,6 +132,7 @@
     yp_dev, ym_dev = place(lax.rem(y + 1, 4), x, z, core), place(lax.rem(y + 3, 4), x, z, core)
     flip_dev = place(y, 3 - x, z, core)
     side_dev = place(y, 2 * x_hi + 1 - x_lo, z, core)
+    up_across_dev, down_across_dev = place(lax.rem(y + 1, 4), 3 - x, z, core), place(lax.rem(y + 3, 4), 3 - x, z, core)
 
     def remote(src, dst, send_sem, recv_sem, device):
         return pltpu.make_async_remote_copy(
@@ -148,23 +149,95 @@
         pltpu.make_async_copy(wq_ref.at[0], wq.at[x_hi], load_sem.at[0]),
         pltpu.make_async_copy(wo_ref.at[0], wo.at[x_hi], load_sem.at[1]),
     ]
-    load_in = pltpu.make_async_copy(inputs_ref.at[0, x_hi, 0], hidden.at[0], load_sem.at[2])
-    load_cot = pltpu.make_async_copy(cotangent_ref.at[0, x_hi, 0], upstream.at[2, 0:SEQ], load_sem.at[3])
+    load_in = pltpu.make_async_copy(inputs_ref.at[0, 0, 0], hidden.at[0], load_sem.at[2])
+    load_cot = pltpu.make_async_copy(cotangent_ref.at[0, 0, 0], upstream.at[2, 0:SEQ], load_sem.at[3])
+    load_entry = [pltpu.make_async_copy(inputs_ref.at[0, s, 0], entry.at[s], load_sem.at[4 + s]) for s in range(2)]
     for copy in loads:
         copy.start()
 
+    near, far = x_hi == 0, x_hi == 1
+
+    @pl.when((y == 0) & near)
+    def _():
+        load_entry[0].start()
+        load_entry[1].start()
+        load_in.start()
+
+    @pl.when((y == 3) & near)
+    def _():
+        load_cot.start()
+
+    barrier = pltpu.get_barrier_semaphore()
+    for device in (core_dev, xp_dev, xm_dev, zp_dev, zm_dev, yp_dev, ym_dev, up_across_dev, down_across_dev):
+        pl.semaphore_signal(barrier, inc=1, device_id=device, device_id_type=MESH)
+    pl.semaphore_wait(barrier, 9)
+
+    in_hop = remote(inputs_ref.at[0, 1, 0], hidden.at[0], hop_send.at[2], hop_recv.at[2], side_dev)
+    cot_hop = remote(cotangent_ref.at[0, 1, 0], upstream.at[2, 0:SEQ], hop_send.at[3], hop_recv.at[3], side_dev)
+
+    @pl.when((y == 0) & far)
+    def _():
+        in_hop.start()
+
+    @pl.when((y == 3) & far)
+    def _():
+        cot_hop.start()
+
+    h_hop = remote(hidden.at[2], hidden.at[0], hop_send.at[0], hop_recv.at[0], yp_dev)
+    c_hop = remote(upstream.at[0, 0:SEQ], upstream.at[2, 0:SEQ], hop_send.at[1], hop_recv.at[1], ym_dev)
+
+    def run_forward(h, weights, layer):
+        wide = h.astype(F32)
+        inverse = inverse_norm(wide)
+        normed[layer, 0:SEQ] = (wide * inverse).astype(BF16)
+        joined[layer] = (mm(h, wq[weights]) * inverse).astype(BF16)
+        attention_forward(joined[layer], probs, att, layer)
+        return (wide + mm_nt(att[layer, 0:SEQ], wo[weights])).astype(BF16)
+
+    across = [remote(passed.at[s], entry.at[s], entry_send.at[s], entry_recv.at[s], flip_dev) for s in range(2)]
+    onward = [
+        remote(passed.at[0], hidden.at[0], entry_send.at[0], hop_recv.at[0], up_across_dev),
+        remote(passed.at[1], hidden.at[0], entry_send.at[1], hop_recv.at[0], yp_dev),
+    ]
+
     @pl.when(y == 0)
     def _():
-        load_in.start()
-
-    @pl.when(y == 3)
-    def _():
-        load_cot.start()
-
-    barrier = pltpu.get_barrier_semaphore()
-    for device in (core_dev, xp_dev, xm_dev, zp_dev, zm_dev, yp_dev, ym_dev):
-        pl.semaphore_signal(barrier, inc=1, device_id=device, device_id_type=MESH)
-    pl.semaphore_wait(barrier, 7)
+        for copy in loads:
+            copy.wait()
+
+        def first_pass(s, carry):
+            for k in range(2):
+                @pl.when((s == k) & near)
+                def _():
+                    load_entry[k].wait()
+
+                @pl.when((s == k) & far)
+                def _():
+                    across[k].wait_recv()
+
+            passed[s] = run_forward(entry[s], x_hi, 0)
+            for k in range(2):
+                @pl.when((s == k) & near)
+                def _():
+                    across[k].start()
+
+                @pl.when((s == k) & far)
+                def _():
+                    onward[k].start()
+
+            return carry
+
+        lax.fori_loop(0, 2, first_pass, 0)
+
+        @pl.when(near)
+        def _():
+            for copy in across:
+                copy.wait_send()
+
+        @pl.when(far)
+        def _():
+            for copy in onward:
+                copy.wait_send()
 
     other = 1 - x_hi
     piece = lax.rem(z + 2 * x_lo, 4)
@@ -211,33 +284,31 @@
         for k in range(4):
             block = chunk(wq, wo, other, pieces[k], 1 - core, part)
             remote(block, block, core_send.at[part, k], core_recv.at[part, k], core_dev).wait_recv()
-    for copy in loads:
-        copy.wait()
-
-    h_hop = remote(hidden.at[2], hidden.at[0], hop_send.at[0], hop_recv.at[0], yp_dev)
-    c_hop = remote(upstream.at[0, 0:SEQ], upstream.at[2, 0:SEQ], hop_send.at[1], hop_recv.at[1], ym_dev)
-
-    @pl.when(y == 0)
+
+    @pl.when(y > 0)
+    def _():
+        for copy in loads:
+            copy.wait()
+
+    @pl.when((y == 0) & near)
     def _():
         load_in.wait()
 
+    @pl.when((y == 0) & far)
+    def _():
+        in_hop.wait()
+
     @pl.when(y > 0)
     def _():
         h_hop.wait_recv()
 
     def forward(layer, carry):
-        h = hidden[layer]
-        wide = h.astype(F32)
-        inverse = inverse_norm(wide)
-        normed[layer, 0:SEQ] = (wide * inverse).astype(BF16)
-        joined[layer] = (mm(h, wq[layer]) * inverse).astype(BF16)
-        attention_forward(joined[layer], probs, att, layer)
-        hidden[layer + 1] = (wide + mm_nt(att[layer, 0:SEQ], wo[layer])).astype(BF16)
+        hidden[layer + 1] = run_forward(hidden[layer], layer, layer)
         return carry
 
     lax.fori_loop(0, 2, forward, 0)
 
-    @pl.when(y < 3)
+    @pl.when((y > 0) & (y < 3))
     def _():
         h_hop.start()
 
@@ -248,9 +319,13 @@
     for number in range(4):
         share(*shared[number], number)
 
-    @pl.when(y == 3)
+    @pl.when((y == 3) & near)
     def _():
         load_cot.wait()
+
+    @pl.when((y == 3) & far)
+    def _():
+        cot_hop.wait()
 
     @pl.when(y < 3)
     def _():
@@ -376,7 +451,7 @@
     for copy in sent:
         copy.wait_send()
 
-    @pl.when(y < 3)
+    @pl.when((y > 0) & (y < 3))
     def _():
         h_hop.wait_send()
 
@@ -411,6 +486,8 @@
         scratch_shapes=[
             pltpu.VMEM((2, D, QKV), BF16),
             pltpu.VMEM((2, D, D), BF16),
+            pltpu.VMEM((2, SEQ, D), BF16),
+            pltpu.VMEM((2, SEQ, D), BF16),
             pltpu.VMEM((3, SEQ, D), BF16),
             pltpu.VMEM((2, 2 * SEQ, D), BF16),
             pltpu.VMEM((2, SEQ, QKV), BF16),
@@ -421,7 +498,7 @@
             pltpu.VMEM((4, 4, 64, COLS), BF16),
             *flow(),
             *flow(),
-            dma((4,)),
+            dma((6,)),
             dma((4,)),
             dma((4,)),
             dma((4, 4)),
@@ -430,6 +507,8 @@
             dma((4, 4)),
             dma((2,)),
             dma((2,)),
+            dma((4,)),
+            dma((4,)),
             dma((8,)),
             dma((8,)),
             dma((24,)),

time: 151 us -> 142 us (0.940)
  Pallas kernels: 145 us -> 137 us
    pallas_call x1, Pallas kernels: 145 us -> 137 us  [on_device(): pl.pallas_call(kernel, out_shape=(jax.ShapeDtypeStruct((1, 64, QKV), F32)...]
where the time goes in v2:
time: 142 us; the launch traced here: 141 us
  Pallas kernels  137 us (96%)
  local copies, waits for them, and re-layouts  3.44 us (2%)
    pallas_call x1, Pallas kernels, on_device(): pl.pallas_call(kernel, out_shape=(jax.ShapeDtypeStruct((1, 64, QKV), F32)...  137 us
    unnamed x2, local copies, waits for them, and re-layouts  3.44 us

profile of v2, /device:TPU:0, one launch (start us, length us, event | category | flops | bytes accessed | tf_op | source)
XLA Modules:
  0.0 140.7 jit_solution(14029179407865697143)
XLA Ops:
  0.6 136.7 %shard_map.59 = (f32[1,64,1536]{2,1,0:T(8,128)}, f32[1,64,1024]{2,1,0:T(8,128)}) custom-call(bf16[1,2,1,128,1024]{4,3,2,1,0:T(8,128)(2,1)} %inputs_ref.1, bf16[1,2,1,128,1024]{4,3,2,1,0:T(8,128)(2,1)} %cotangent_ref.1, bf16[1,1024,1536]{2,1,0:T(8,128)(2,1)} %wq_ref.1, bf16[1,1024,1024]{2,1,0:T(8,128)(2,1)} %wo_ref.1), custom_call_target="tpu_custom_call" | custom-call | tf_op jit(solution)/shard_map/pallas_call | solution.py:481
  137.3 1.8 %copy.8 = f32[1,64,1536]{2,1,0:T(8,128)} copy(f32[1,64,1536]{2,1,0:T(8,128)} %get-tuple-element.4) | data formatting | bytes 786432
  139.1 1.7 %copy.9 = f32[1,64,1024]{2,1,0:T(8,128)} copy(f32[1,64,1024]{2,1,0:T(8,128)} %get-tuple-element.5) | data formatting | bytes 524288

commit v3 on v2

--- a/solution.py
+++ b/solution.py
@@ -16,8 +16,9 @@
 SEQ = 128
 QKV = 1536
 COLS = 2560
-HALF = 1280
-QUARTER = 640
+HALF = 768
+QUARTER = 384
+WIDE = 512
 CHUNK = 64
 
 
@@ -66,12 +67,12 @@
         scores = mm_nt(queries, block_diagonal(keys, group)) * 0.125
         exponent = jnp.where(causal, jnp.exp(scores), 0.0)
         left, right = half_sums(exponent)
-        probs = jnp.concatenate([exponent[:, :128] / left, exponent[:, 128:] / right], axis=1).astype(BF16)
+        probs = jnp.concatenate([exponent[:, :128] * (1.0 / left), exponent[:, 128:] * (1.0 / right)], axis=1).astype(BF16)
         probs_ref[layer, group] = probs
         mixed = mm(probs, block_diagonal(values, group)).astype(BF16)
         at = group * 256
-        att_ref[layer, 0:SEQ, at : at + 128] = mixed[:128]
-        att_ref[layer, 0:SEQ, at + 128 : at + 256] = mixed[128:]
+        att_ref[:, at : at + 128] = mixed[:128]
+        att_ref[:, at + 128 : at + 256] = mixed[128:]
 
 
 def attention_backward(joined, d_attention, probs_ref, dj_ref, layer):
@@ -111,17 +112,20 @@
 
 def kernel(
     inputs_ref, cotangent_ref, wq_ref, wo_ref,
-    gq_ref, go_ref,
-    wq, wo, entry, passed, hidden, normed, joined, probs, att, upstream, dj, grads,
+    out_ref,
+    wq, wo, wqt, entry, passed, hidden, normed, joined, probs, att, upstream, dj, c_pack, c_all, grads, grads_out,
     z_a1, z_b1, z_m2, z_p2, z_r, z_sa1, z_sb1, z_sm2, z_sp2,
     x_a1, x_b1, x_m2, x_p2, x_r, x_sa1, x_sb1, x_sm2, x_sp2,
+    o_a1, o_b1, o_m2, o_p2,
     load_sem, flip_send, flip_recv, spread_send, spread_recv, core_send, core_recv,
-    entry_send, entry_recv, hop_send, hop_recv, share_send, share_recv, sum_send, sum_recv,
+    entry_send, entry_recv, hop_send, hop_recv, share_send, share_recv,
+    att_send, att_recv, att_core_send, att_core_recv, c_send, c_recv, sum_send, sum_recv,
 ):
     section, dp = lax.axis_index("section"), lax.axis_index("dp")
     y, x_hi = lax.div(section, 2), lax.rem(section, 2)
     z, x_lo, core = lax.div(dp, 4), lax.rem(lax.div(dp, 2), 2), lax.rem(dp, 2)
     x = 2 * x_hi + x_lo
+    slot = 2 * z + core
 
     def place(y, x, z, core):
         return (2 * y + lax.div(x, 2), 4 * z + 2 * lax.rem(x, 2) + core)
@@ -130,6 +134,7 @@
     xp_dev, xm_dev = place(y, lax.rem(x + 1, 4), z, core), place(y, lax.rem(x + 3, 4), z, core)
     zp_dev, zm_dev = place(y, x, lax.rem(z + 1, 4), core), place(y, x, lax.rem(z + 3, 4), core)
     yp_dev, ym_dev = place(lax.rem(y + 1, 4), x, z, core), place(lax.rem(y + 3, 4), x, z, core)
+    column = [[place(y, x, lax.rem(z + k, 4), c) for c in (core, 1 - core)] for k in range(4)]
     flip_dev = place(y, 3 - x, z, core)
     side_dev = place(y, 2 * x_hi + 1 - x_lo, z, core)
     up_across_dev, down_across_dev = place(lax.rem(y + 1, 4), 3 - x, z, core), place(lax.rem(y + 3, 4), 3 - x, z, core)
@@ -150,7 +155,7 @@
         pltpu.make_async_copy(wo_ref.at[0], wo.at[x_hi], load_sem.at[1]),
     ]
     load_in = pltpu.make_async_copy(inputs_ref.at[0, 0, 0], hidden.at[0], load_sem.at[2])
-    load_cot = pltpu.make_async_copy(cotangent_ref.at[0, 0, 0], upstream.at[2, 0:SEQ], load_sem.at[3])
+    load_cot = pltpu.make_async_copy(cotangent_ref.at[0, 0, 0], upstream.at[2], load_sem.at[3])
     load_entry = [pltpu.make_async_copy(inputs_ref.at[0, s, 0], entry.at[s], load_sem.at[4 + s]) for s in range(2)]
     for copy in loads:
         copy.start()
@@ -168,12 +173,13 @@
         load_cot.start()
 
     barrier = pltpu.get_barrier_semaphore()
-    for device in (core_dev, xp_dev, xm_dev, zp_dev, zm_dev, yp_dev, ym_dev, up_across_dev, down_across_dev):
+    ring = [column[k][c] for k in range(4) for c in range(2) if (k, c) != (0, 0)]
+    for device in (*ring, xp_dev, xm_dev, yp_dev, ym_dev, up_across_dev, down_across_dev):
         pl.semaphore_signal(barrier, inc=1, device_id=device, device_id_type=MESH)
-    pl.semaphore_wait(barrier, 9)
+    pl.semaphore_wait(barrier, 13)
 
     in_hop = remote(inputs_ref.at[0, 1, 0], hidden.at[0], hop_send.at[2], hop_recv.at[2], side_dev)
-    cot_hop = remote(cotangent_ref.at[0, 1, 0], upstream.at[2, 0:SEQ], hop_send.at[3], hop_recv.at[3], side_dev)
+    cot_hop = remote(cotangent_ref.at[0, 1, 0], upstream.at[2], hop_send.at[3], hop_recv.at[3], side_dev)
 
     @pl.when((y == 0) & far)
     def _():
@@ -184,15 +190,15 @@
         cot_hop.start()
 
     h_hop = remote(hidden.at[2], hidden.at[0], hop_send.at[0], hop_recv.at[0], yp_dev)
-    c_hop = remote(upstream.at[0, 0:SEQ], upstream.at[2, 0:SEQ], hop_send.at[1], hop_recv.at[1], ym_dev)
+    c_hop = remote(upstream.at[0], upstream.at[2], hop_send.at[1], hop_recv.at[1], ym_dev)
 
     def run_forward(h, weights, layer):
         wide = h.astype(F32)
         inverse = inverse_norm(wide)
         normed[layer, 0:SEQ] = (wide * inverse).astype(BF16)
         joined[layer] = (mm(h, wq[weights]) * inverse).astype(BF16)
-        attention_forward(joined[layer], probs, att, layer)
-        return (wide + mm_nt(att[layer, 0:SEQ], wo[weights])).astype(BF16)
+        attention_forward(joined[layer], probs, att.at[layer, slot], layer)
+        return (wide + mm_nt(att[layer, slot], wo[weights])).astype(BF16)
 
     across = [remote(passed.at[s], entry.at[s], entry_send.at[s], entry_recv.at[s], flip_dev) for s in range(2)]
     onward = [
@@ -285,10 +291,22 @@
             block = chunk(wq, wo, other, pieces[k], 1 - core, part)
             remote(block, block, core_send.at[part, k], core_recv.at[part, k], core_dev).wait_recv()
 
+    def transpose_weights():
+        def one(k, carry):
+            layer, cols = lax.div(k, 6), pl.ds(pl.multiple_of(lax.rem(k, 6) * 256, 256), 256)
+            wqt[layer, cols] = wq[layer, :, cols].T
+            return carry
+
+        lax.fori_loop(0, 12, one, 0)
+
     @pl.when(y > 0)
     def _():
         for copy in loads:
             copy.wait()
+
+    @pl.when(y >= 2)
+    def _():
+        transpose_weights()
 
     @pl.when((y == 0) & near)
     def _():
@@ -312,12 +330,80 @@
     def _():
         h_hop.start()
 
-    def share(buf, slot, number):
-        go(remote(buf.at[slot, 0:SEQ], buf.at[slot, SEQ : 2 * SEQ], share_send.at[number], share_recv.at[number], core_dev))
-
-    shared = [(normed, 0), (normed, 1), (att, 0), (att, 1), (upstream, 2), (upstream, 1), (dj, 1), (dj, 0)]
-    for number in range(4):
-        share(*shared[number], number)
+    def share(buf, layer, number):
+        return remote(
+            buf.at[layer, 0:SEQ], buf.at[layer, SEQ : 2 * SEQ], share_send.at[number], share_recv.at[number], core_dev
+        )
+
+    shares = [share(normed, 0, 0), share(normed, 1, 1), share(dj, 0, 2), share(dj, 1, 3)]
+    sent.extend(shares)
+
+    def att_copy(layer, k, to_core=False):
+        if to_core:
+            block = att.at[layer, 2 * lax.rem(z + 4 - k, 4) + core]
+            return remote(block, block, att_core_send.at[layer, k], att_core_recv.at[layer, k], core_dev)
+        block = att.at[layer, slot]
+        return remote(block, block, att_send.at[layer, k], att_recv.at[layer, k], column[k][0])
+
+    spread_att = [att_copy(layer, k) for layer in (1, 0) for k in (1, 3, 2)]
+    core_att = [att_copy(layer, k, True) for layer in (1, 0) for k in (0, 1, 3, 2)]
+    sent.extend(spread_att + core_att)
+
+    def send_attention():
+        shares[0].start()
+        shares[1].start()
+        for copy in spread_att:
+            copy.start()
+
+    def pass_attention():
+        for layer in (1, 0):
+            for k in (0, 1, 3, 2):
+                if k:
+                    block = att.at[layer, 2 * lax.rem(z + 4 - k, 4) + core]
+                    remote(block, block, att_send.at[layer, k], att_recv.at[layer, k], core_dev).wait_recv()
+                att_copy(layer, k, True).start()
+
+    def await_attention(layer):
+        for k in range(4):
+            block = att.at[layer, 2 * lax.rem(z + 4 - k, 4) + 1 - core]
+            remote(block, block, att_core_send.at[layer, k], att_core_recv.at[layer, k], core_dev).wait_recv()
+
+    def c_copy(layer, k, c):
+        source = c_pack.at[layer, core if c == 0 else 1 - core, lax.rem(z + k, 4)]
+        return remote(source, c_all.at[layer, slot], c_send.at[layer, 2 * k + c], c_recv.at[layer, 2 * k + c], column[k][c])
+
+    def send_c(layer):
+        low = lax.broadcasted_iota(jnp.int32, (SEQ, 128), 1) < 64
+        for to in range(4):
+            a = upstream[layer + 1, :, 256 * to : 256 * to + 128].astype(F32)
+            b = upstream[layer + 1, :, 256 * to + 128 : 256 * to + 256].astype(F32)
+            c_pack[layer, 0, to] = jnp.where(low, a, pltpu.roll(b, 64, 1)).astype(BF16)
+            c_pack[layer, 1, to] = jnp.where(low, pltpu.roll(a, 64, 1), b).astype(BF16)
+        c_all[layer, slot] = c_pack[layer, core, z]
+        for k in (1, 3, 2, 0):
+            for c in range(2):
+                if (k, c) != (0, 0):
+                    c_copy(layer, k, c).start()
+
+    def await_c(layer):
+        for k in range(4):
+            for c in range(2):
+                if (k, c) != (0, 0):
+                    block = c_all.at[layer, 2 * lax.rem(z + 4 - k, 4) + (core if c == 0 else 1 - core)]
+                    remote(
+                        block, block, c_send.at[layer, 2 * k + c], c_recv.at[layer, 2 * k + c], core_dev
+                    ).wait_recv()
+
+    sent.extend(c_copy(layer, k, c) for layer in range(2) for k in range(4) for c in range(2) if (k, c) != (0, 0))
+
+    @pl.when(y < 3)
+    def _():
+        send_attention()
+
+    @pl.when(y < 2)
+    def _():
+        transpose_weights()
+        pass_attention()
 
     @pl.when((y == 3) & near)
     def _():
@@ -330,18 +416,32 @@
     @pl.when(y < 3)
     def _():
         c_hop.wait_recv()
+
+    def run_backward(layer):
+        c = upstream[layer + 1]
+        d_attention = mm(c, wo[layer]).astype(BF16)
+        attention_backward(joined[layer], d_attention, probs, dj, layer)
+
+        @pl.when((layer > 0) | (y > 0))
+        def _():
+            d_normed = mm(dj[layer, 0:SEQ], wqt[layer])
+            wide = hidden[layer].astype(F32)
+            inverse = inverse_norm(wide)
+            scaled = wide * inverse
+            along = jnp.mean(d_normed * scaled, axis=-1, keepdims=True)
+            upstream[layer] = (
+                upstream[layer + 1].astype(F32) + inverse * (d_normed - scaled * along)
+            ).astype(BF16)
 
     def backward(step, carry):
         layer = 1 - step
-        c = upstream[layer + 1, 0:SEQ]
-        d_attention = mm(c, wo[layer]).astype(BF16)
-        attention_backward(joined[layer], d_attention, probs, dj, layer)
-        d_normed = mm_nt(dj[layer, 0:SEQ], wq[layer])
-        wide = hidden[layer].astype(F32)
-        inverse = inverse_norm(wide)
-        scaled = wide * inverse
-        along = jnp.mean(d_normed * scaled, axis=-1, keepdims=True)
-        upstream[layer, 0:SEQ] = (c.astype(F32) + inverse * (d_normed - scaled * along)).astype(BF16)
+
+        @pl.when(y == 0)
+        def _():
+            send_c(layer)
+
+        run_backward(layer)
+        share(dj, layer, 2 + layer).start()
         return carry
 
     lax.fori_loop(0, 2, backward, 0)
@@ -350,12 +450,9 @@
     def _():
         c_hop.start()
 
-    for number in range(4, 8):
-        share(*shared[number], number)
-    for number, (buf, slot) in enumerate(shared):
-        remote(
-            buf.at[slot, 0:SEQ], buf.at[slot, SEQ : 2 * SEQ], share_send.at[number], share_recv.at[number], core_dev
-        ).wait_recv()
+    @pl.when(y == 3)
+    def _():
+        send_attention()
 
     low = lax.broadcasted_iota(jnp.int32, (2 * SEQ, 128), 1) < 64
 
@@ -372,42 +469,69 @@
                 tiles.append(jnp.where(low, first, second).astype(BF16))
         return jnp.concatenate(tiles, axis=1)
 
-    for layer in (1, 0):
+    def gradient(layer):
         left = own_columns(normed[layer])
         for lo in range(2):
             part = mm_tn(left[:, 256 * lo : 256 * lo + 256], dj[layer]).astype(BF16)
-            grads[2 * layer + lo, :, :, 0:QKV] = part.reshape(4, 64, QKV)
-        left = own_columns(upstream[layer + 1])
-        for lo in range(2):
-            part = mm_tn(left[:, 256 * lo : 256 * lo + 256], att[layer]).astype(BF16)
-            grads[2 * layer + lo, :, :, QKV:COLS] = part.reshape(4, 64, D)
-
-    def ring_sum(view, position, plus, minus, bufs, sems):
+            grads[2 * layer + lo] = part.reshape(4, 64, QKV)
+
+    def gradient_out(layer):
+        await_c(layer)
+        await_attention(layer)
+        part = mm_tn(c_all[layer].reshape(8 * SEQ, 128), att[layer].reshape(8 * SEQ, D)).astype(BF16)
+        grads_out[2 * layer : 2 * layer + 2] = part.reshape(2, 64, D)
+
+    def ring_sum(view, position, plus, minus, bufs, sems, layers=None):
         a1, b1, m2, p2, alpha, beta = bufs
         opposite, after, before = (lax.rem(position + k, 4) for k in (2, 1, 3))
         s, r = sum_send.at, sum_recv.at
-
-        def first():
-            go(remote(view(opposite, 0), a1, s[sems], r[sems], plus))
-            go(remote(view(opposite, 1), b1, s[sems + 1], r[sems + 1], minus))
-            go(remote(view(after, 1), m2.at[beta], s[sems + 2], r[sems + 2], plus))
-            go(remote(view(before, 0), p2.at[alpha], s[sems + 3], r[sems + 3], minus))
-
-        def second():
-            mine = view(after, 0)
-            remote(mine, a1, s[sems], r[sems], plus).wait_recv()
-            mine[...] = (mine[...].astype(F32) + a1[...].astype(F32)).astype(BF16)
-            go(remote(mine, m2.at[alpha], s[sems + 4], r[sems + 4], plus))
-            mine = view(before, 1)
-            remote(mine, b1, s[sems + 1], r[sems + 1], minus).wait_recv()
-            mine[...] = (mine[...].astype(F32) + b1[...].astype(F32)).astype(BF16)
-            go(remote(mine, p2.at[beta], s[sems + 5], r[sems + 5], minus))
+        copies = [
+            remote(view(opposite, 0), a1, s[sems], r[sems], plus),
+            remote(view(opposite, 1), b1, s[sems + 1], r[sems + 1], minus),
+            remote(view(after, 1), m2.at[beta], s[sems + 2], r[sems + 2], plus),
+            remote(view(before, 0), p2.at[alpha], s[sems + 3], r[sems + 3], minus),
+            remote(view(after, 0), m2.at[alpha], s[sems + 4], r[sems + 4], plus),
+            remote(view(before, 1), p2.at[beta], s[sems + 5], r[sems + 5], minus),
+        ]
+        sent.extend(copies)
+
+        def only(stage, target):
+            if stage is None:
+                return lambda body: body()
+            return pl.when(layers(target) == stage)
+
+        def first(stage=None):
+            @only(stage, opposite)
+            def _():
+                copies[0].start()
+                copies[1].start()
+
+            @only(stage, after)
+            def _():
+                copies[2].start()
+
+            @only(stage, before)
+            def _():
+                copies[3].start()
+
+        def second(stage=None):
+            @only(stage, after)
+            def _():
+                mine = view(after, 0)
+                copies[0].wait_recv()
+                mine[...] = (mine[...].astype(F32) + a1[...].astype(F32)).astype(BF16)
+                copies[4].start()
+
+            @only(stage, before)
+            def _():
+                mine = view(before, 1)
+                copies[1].wait_recv()
+                mine[...] = (mine[...].astype(F32) + b1[...].astype(F32)).astype(BF16)
+                copies[5].start()
 
         def last():
-            remote(view(after, 1), m2.at[beta], s[sems + 2], r[sems + 2], plus).wait_recv()
-            remote(view(before, 0), p2.at[alpha], s[sems + 3], r[sems + 3], minus).wait_recv()
-            remote(view(after, 0), m2.at[alpha], s[sems + 4], r[sems + 4], plus).wait_recv()
-            remote(view(before, 1), p2.at[beta], s[sems + 5], r[sems + 5], minus).wait_recv()
+            for copy in copies[2:]:
+                copy.wait_recv()
 
         return first, second, last
 
@@ -417,36 +541,80 @@
     z_cols, x_cols, own_cols = halves(0), halves(HALF), halves(0)
     wide_at = [(slice(None), slice(None), cols) for cols in own_cols]
     flat_at = [(slice(None), cols) for cols in own_cols]
-    z_big = ring_sum(
-        lambda t, k: grads.at[:, t, :, z_cols[k]], z, zp_dev, zm_dev, (z_a1, z_b1, z_m2, z_p2, *wide_at), 0
-    )
+
+    def z_ring(layer):
+        pair = pl.ds(2 * layer, 2)
+        bufs = (z_a1.at[pair], z_b1.at[pair], z_m2.at[pair], z_p2.at[pair], *wide_at)
+        return ring_sum(lambda t, k: grads.at[pair, t, :, z_cols[k]], z, zp_dev, zm_dev, bufs, 24 if layer else 0)
+
+    z_big = [z_ring(0), z_ring(1)]
+    def layer_of(target):
+        return lax.div(target, 2)
+
     x_big = ring_sum(
-        lambda t, k: grads.at[t, :, :, x_cols[k]], x, xp_dev, xm_dev, (x_a1, x_b1, x_m2, x_p2, *wide_at), 6
+        lambda t, k: grads.at[t, :, :, x_cols[k]], x, xp_dev, xm_dev, (x_a1, x_b1, x_m2, x_p2, *wide_at), 6, layer_of
     )
     z_small = ring_sum(
-        lambda t, k: z_r.at[t, :, own_cols[k]], x, xp_dev, xm_dev, (z_sa1, z_sb1, z_sm2, z_sp2, *flat_at), 12
+        lambda t, k: z_r.at[t, :, own_cols[k]], x, xp_dev, xm_dev, (z_sa1, z_sb1, z_sm2, z_sp2, *flat_at), 12, layer_of
     )
     x_small = ring_sum(
         lambda t, k: x_r.at[t, :, own_cols[k]], z, zp_dev, zm_dev, (x_sa1, x_sb1, x_sm2, x_sp2, *flat_at), 18
     )
-    z_big[0]()
-    x_big[0]()
-    z_big[1]()
-    x_big[1]()
-    z_big[2]()
-    z_r[...] = (grads[:, z, :, 0:HALF].astype(F32) + z_m2[...].astype(F32) + z_p2[...].astype(F32)).astype(BF16)
-    z_small[0]()
+    out_at = [(slice(None), pl.ds(0, WIDE)), (slice(None), pl.ds(WIDE, WIDE))]
+    o_ring = ring_sum(
+        lambda t, k: grads_out.at[t, :, pl.ds(k * WIDE, WIDE)], x, xp_dev, xm_dev, (o_a1, o_b1, o_m2, o_p2, *out_at), 30
+    )
+
+    def sum_z(layer):
+        pair = slice(2 * layer, 2 * layer + 2)
+        z_r[pair] = (grads[pair, z, :, 0:HALF].astype(F32) + z_m2[pair].astype(F32) + z_p2[pair].astype(F32)).astype(BF16)
+
+    shares[1].wait_recv()
+    shares[3].wait_recv()
+    gradient(1)
+    z_big[1][0]()
+    x_big[0](1)
+    shares[0].wait_recv()
+    shares[2].wait_recv()
+    gradient(0)
+    z_big[0][0]()
+    x_big[0](0)
+
+    @pl.when(y > 0)
+    def _():
+        send_c(1)
+        send_c(0)
+
+    @pl.when(y >= 2)
+    def _():
+        pass_attention()
+
+    gradient_out(1)
+    gradient_out(0)
+    o_ring[0]()
+    z_big[1][1]()
+    x_big[1](1)
+    z_big[0][1]()
+    x_big[1](0)
+    z_big[1][2]()
+    sum_z(1)
+    z_small[0](1)
+    o_ring[1]()
+    z_big[0][2]()
+    sum_z(0)
+    z_small[0](0)
     x_big[2]()
-    x_r[...] = (grads[x, :, :, HALF:COLS].astype(F32) + x_m2[...].astype(F32) + x_p2[...].astype(F32)).astype(BF16)
+    x_r[...] = (grads[x, :, :, HALF:QKV].astype(F32) + x_m2[...].astype(F32) + x_p2[...].astype(F32)).astype(BF16)
     x_small[0]()
-    z_small[1]()
+    z_small[1](1)
+    z_small[1](0)
     x_small[1]()
+    o_ring[2]()
+    out_ref[:, QKV:COLS] = grads_out[x].astype(F32) + o_m2[...].astype(F32) + o_p2[...].astype(F32)
     z_small[2]()
-    gq_ref[0, :, 0:HALF] = z_r[x].astype(F32) + z_sm2[...].astype(F32) + z_sp2[...].astype(F32)
+    out_ref[:, 0:HALF] = z_r[x].astype(F32) + z_sm2[...].astype(F32) + z_sp2[...].astype(F32)
     x_small[2]()
-    total = x_r[z].astype(F32) + x_sm2[...].astype(F32) + x_sp2[...].astype(F32)
-    gq_ref[0, :, HALF:QKV] = total[:, : QKV - HALF]
-    go_ref[0] = total[:, QKV - HALF :]
+    out_ref[:, HALF:QKV] = x_r[z].astype(F32) + x_sm2[...].astype(F32) + x_sp2[...].astype(F32)
 
     for copy in sent:
         copy.wait_send()
@@ -478,26 +646,34 @@
             pltpu.VMEM((64, HALF), BF16),
         ]
 
-    return pl.pallas_call(
+    total = pl.pallas_call(
         kernel,
-        out_shape=(jax.ShapeDtypeStruct((1, 64, QKV), F32), jax.ShapeDtypeStruct((1, 64, D), F32)),
+        out_shape=jax.ShapeDtypeStruct((64, COLS), F32),
         in_specs=[any_space] * 4,
-        out_specs=(vmem, vmem),
+        out_specs=vmem,
         scratch_shapes=[
             pltpu.VMEM((2, D, QKV), BF16),
             pltpu.VMEM((2, D, D), BF16),
+            pltpu.VMEM((2, QKV, D), BF16),
             pltpu.VMEM((2, SEQ, D), BF16),
             pltpu.VMEM((2, SEQ, D), BF16),
             pltpu.VMEM((3, SEQ, D), BF16),
             pltpu.VMEM((2, 2 * SEQ, D), BF16),
             pltpu.VMEM((2, SEQ, QKV), BF16),
             pltpu.VMEM((2, 4, 256, 256), BF16),
-            pltpu.VMEM((2, 2 * SEQ, D), BF16),
-            pltpu.VMEM((3, 2 * SEQ, D), BF16),
+            pltpu.VMEM((2, 8, SEQ, D), BF16),
+            pltpu.VMEM((3, SEQ, D), BF16),
             pltpu.VMEM((2, 2 * SEQ, QKV), BF16),
-            pltpu.VMEM((4, 4, 64, COLS), BF16),
+            pltpu.VMEM((2, 2, 4, SEQ, 128), BF16),
+            pltpu.VMEM((2, 8, SEQ, 128), BF16),
+            pltpu.VMEM((4, 4, 64, QKV), BF16),
+            pltpu.VMEM((4, 64, D), BF16),
             *flow(),
             *flow(),
+            pltpu.VMEM((64, WIDE), BF16),
+            pltpu.VMEM((64, WIDE), BF16),
+            pltpu.VMEM((64, D), BF16),
+            pltpu.VMEM((64, D), BF16),
             dma((6,)),
             dma((4,)),
             dma((4,)),
@@ -509,15 +685,22 @@
             dma((2,)),
             dma((4,)),
             dma((4,)),
-            dma((8,)),
-            dma((8,)),
-            dma((24,)),
-            dma((24,)),
+            dma((4,)),
+            dma((4,)),
+            dma((2, 4)),
+            dma((2, 4)),
+            dma((2, 4)),
+            dma((2, 4)),
+            dma((2, 8)),
+            dma((2, 8)),
+            dma((36,)),
+            dma((36,)),
         ],
         compiler_params=pltpu.CompilerParams(
             collective_id=0, has_side_effects=True, vmem_limit_bytes=56 * 2**20
         ),
     )(inputs, cotangent, w_qkv, w_out)
+    return (total[None, :, :QKV], total[None, :, QKV:])
 
 
 def solution(mesh):

time: 142 us -> 134 us (0.944)
  Pallas kernels: 137 us -> 129 us
    pallas_call x1, Pallas kernels: 137 us -> 129 us  [on_device(): pl.pallas_call(kernel, out_shape=jax.ShapeDtypeStruct((64, COLS), F32), i...]
    broadcast_in_dim x0 -> x2, local copies, waits for them, and re-layouts: none -> 3.44 us  [on_device(): return (total[None, :, :QKV], total[None, :, QKV:])]
    unnamed x2 -> x0, local copies, waits for them, and re-layouts: 3.44 us -> none
where the time goes in v3:
time: 134 us; the launch traced here: 133 us
  Pallas kernels  129 us (96%)
  local copies, waits for them, and re-layouts  3.44 us (3%)
    pallas_call x1, Pallas kernels, on_device(): pl.pallas_call(kernel, out_shape=jax.ShapeDtypeStruct((64, COLS), F32), i...  129 us
    broadcast_in_dim x2, local copies, waits for them, and re-layouts, on_device(): return (total[None, :, :QKV], total[None, :, QKV:])  3.44 us

profile of v3, /device:TPU:0, one launch (start us, length us, event | category | flops | bytes accessed | tf_op | source)
XLA Modules:
  0.0 133.4 jit_solution(1636126690721301162)
XLA Ops:
  0.6 129.3 %shard_map.59 = f32[64,2560]{1,0:T(8,128)} custom-call(bf16[1,2,1,128,1024]{4,3,2,1,0:T(8,128)(2,1)} %inputs_ref.1, bf16[1,2,1,128,1024]{4,3,2,1,0:T(8,128)(2,1)} %cotangent_ref.1, bf16[1,1024,1536]{2,1,0:T(8,128)(2,1)} %wq_ref.1, bf16[1,1024,1024]{2,1,0:T(8,128)(2,1)} %wo_ref.1), custom_call_target="tpu_custom_call" | custom-call | tf_op jit(solution)/shard_map/pallas_call | solution.py:649
  129.9 1.7 %slice_bitcast_fusion.1 = f32[1,64,1024]{2,1,0:T(8,128)} fusion(f32[64,2560]{1,0:T(8,128)} %shard_map.59), kind=kLoop, calls=%fused_computation.1 | loop fusion | bytes 524288 | tf_op jit(solution)/shard_map/broadcast_in_dim | solution.py:703
  131.6 1.8 %slice_bitcast_fusion = f32[1,64,1536]{2,1,0:T(8,128)} fusion(f32[64,2560]{1,0:T(8,128)} %shard_map.59), kind=kLoop, calls=%fused_computation | loop fusion | bytes 786432 | tf_op jit(solution)/shard_map/broadcast_in_dim | solution.py:703

commit v4 on v3

--- a/solution.py
+++ b/solution.py
@@ -19,7 +19,7 @@
 HALF = 768
 QUARTER = 384
 WIDE = 512
-CHUNK = 64
+PARTS = [("q", k, 32) for k in range(4)] + [("o", k, 64) for k in range(2)]
 
 
 def mm(a, b):
@@ -75,22 +75,27 @@
         att_ref[:, at + 128 : at + 256] = mixed[128:]
 
 
-def attention_backward(joined, d_attention, probs_ref, dj_ref, layer):
+def attention_backward(joined, d_attention, probs_ref, dj_ref, carried, layer, half):
+    at = 64 * half
+    rows = pl.ds(at, 64)
+    early, late = slice(0, 64), slice(64, 128)
     d_keys, d_values = [], []
     for group in range(4):
-        queries = stack_pairs(joined, group)
+        queries = stack_pairs(joined[at : at + 64], group)
         d_heads = stack_pairs(d_attention, group)
         keys, values = kv_pairs(joined, group)
-        probs = probs_ref[layer, group]
+        probs = jnp.concatenate(
+            [probs_ref[layer, group, at : at + 64], probs_ref[layer, group, 128 + at : 192 + at]], axis=0
+        )
         d_probs = mm_nt(d_heads, block_diagonal(values, group))
         wide = probs.astype(F32)
         left, right = half_sums(wide * d_probs)
         centred = jnp.concatenate([d_probs[:, :128] - left, d_probs[:, 128:] - right], axis=1)
         d_scores = (wide * centred * 0.125).astype(BF16)
         d_queries = mm(d_scores, block_diagonal(keys, group)).astype(BF16)
-        at = group * 256
-        dj_ref[layer, 0:SEQ, at : at + 128] = d_queries[:128]
-        dj_ref[layer, 0:SEQ, at + 128 : at + 256] = d_queries[128:]
+        lane = group * 256
+        dj_ref[layer, rows, lane : lane + 128] = d_queries[:64]
+        dj_ref[layer, rows, lane + 128 : lane + 256] = d_queries[64:]
         d_keys.append(mm_tn(d_scores, queries))
         d_values.append(mm_tn(probs, d_heads))
     low = lax.broadcasted_iota(jnp.int32, (128, 128), 1) < 64
@@ -98,12 +103,17 @@
     def merged(even, odd):
         first = even[:128] + pltpu.roll(even[128:], 64, 1)
         second = pltpu.roll(odd[:128], 64, 1) + odd[128:]
-        return jnp.where(low, first, second).astype(BF16)
-
-    for pair in range(2):
-        at = D + pair * 128
-        dj_ref[layer, 0:SEQ, at : at + 128] = merged(d_keys[2 * pair], d_keys[2 * pair + 1])
-        dj_ref[layer, 0:SEQ, at + 256 : at + 384] = merged(d_values[2 * pair], d_values[2 * pair + 1])
+        return jnp.where(low, first, second)
+
+    for number, parts in ((0, d_keys), (1, d_values)):
+        for pair in range(2):
+            total = merged(parts[2 * pair], parts[2 * pair + 1])
+            lane = D + 256 * number + 128 * pair
+            if half:
+                carried[layer, number, pair] = total[early]
+                dj_ref[layer, rows, lane : lane + 128] = total[late].astype(BF16)
+            else:
+                dj_ref[layer, rows, lane : lane + 128] = (total[early] + carried[layer, number, pair]).astype(BF16)
 
 
 def inverse_norm(wide):
@@ -113,7 +123,7 @@
 def kernel(
     inputs_ref, cotangent_ref, wq_ref, wo_ref,
     out_ref,
-    wq, wo, wqt, entry, passed, hidden, normed, joined, probs, att, upstream, dj, c_pack, c_all, grads, grads_out,
+    wq, wo, wqt, entry, passed, hidden, normed, joined, probs, att, upstream, dj, carried, c_pack, c_all, grads, grads_out,
     z_a1, z_b1, z_m2, z_p2, z_r, z_sa1, z_sb1, z_sm2, z_sp2,
     x_a1, x_b1, x_m2, x_p2, x_r, x_sa1, x_sb1, x_sm2, x_sp2,
     o_a1, o_b1, o_m2, o_p2,
@@ -190,7 +200,13 @@
         cot_hop.start()
 
     h_hop = remote(hidden.at[2], hidden.at[0], hop_send.at[0], hop_recv.at[0], yp_dev)
-    c_hop = remote(upstream.at[0], upstream.at[2], hop_send.at[1], hop_recv.at[1], ym_dev)
+    c_hop = [
+        remote(
+            upstream.at[0, 64 * half : 64 * half + 64], upstream.at[2, 64 * half : 64 * half + 64],
+            hop_send.at[(1, 4)[half]], hop_recv.at[(1, 4)[half]], ym_dev,
+        )
+        for half in range(2)
+    ]
 
     def run_forward(h, weights, layer):
         wide = h.astype(F32)
@@ -249,47 +265,44 @@
     piece = lax.rem(z + 2 * x_lo, 4)
     pieces = [lax.rem(piece + k, 4) for k in range(4)]
 
-    def chunk_rows(which, half, part):
-        return pl.ds(pl.multiple_of(which * 256 + half * 128 + (part % 2) * CHUNK, CHUNK), CHUNK)
-
-    def chunk(buf_q, buf_o, slot, which, half, part):
-        rows = chunk_rows(which, half, part)
-        return (buf_q if part < 2 else buf_o).at[slot, rows]
-
-    for part in range(4):
-        src = chunk(wq_ref, wo_ref, 0, pieces[2], core, part)
-        go(remote(src, chunk(wq, wo, x_hi, pieces[2], core, part), flip_send.at[part], flip_recv.at[part], flip_dev))
-
-    def await_flip(part):
-        block = chunk(wq, wo, other, pieces[0], core, part)
-        remote(block, block, flip_send.at[part], flip_recv.at[part], flip_dev).wait_recv()
-
-    def spread(part):
-        block = chunk(wq, wo, other, pieces[0], core, part)
-        for slot, device in ((1, zm_dev), (2, side_dev), (3, zp_dev)):
-            go(remote(block, block, spread_send.at[part, slot], spread_recv.at[part, slot], device))
-
-    def to_core(part, k):
-        block = chunk(wq, wo, other, pieces[k], core, part)
-        go(remote(block, block, core_send.at[part, k], core_recv.at[part, k], core_dev))
-
-    def gather_rest(part):
+    def chunk(buf, slot, which, half, part):
+        name, k, rows = part
+        at = (half * 4 + which) * 128 + k * rows
+        return buf[name].at[slot, pl.ds(pl.multiple_of(at, rows), rows)]
+
+    held, given = {"q": wq, "o": wo}, {"q": wq_ref, "o": wo_ref}
+
+    def flip_copy(i, block, source=None):
+        return remote(block if source is None else source, block, flip_send.at[i], flip_recv.at[i], flip_dev)
+
+    for i, part in enumerate(PARTS):
+        go(flip_copy(i, chunk(held, x_hi, pieces[2], core, part), chunk(given, 0, pieces[2], core, part)))
+
+    def spread(i, part):
+        flip_copy(i, chunk(held, other, pieces[0], core, part)).wait_recv()
+        block = chunk(held, other, pieces[0], core, part)
+        for k, device in ((1, zm_dev), (2, side_dev), (3, zp_dev)):
+            go(remote(block, block, spread_send.at[i, k], spread_recv.at[i, k], device))
+
+    def core_copy(i, part, half):
+        name, k, rows = part
+        block = held[name].at[other].reshape(8, 128, held[name].shape[2])
+        block = block.at[pl.ds(half * 4, 4), pl.ds(k * rows, rows)]
+        return remote(block, block, core_send.at[i], core_recv.at[i], core_dev)
+
+    def gather_rest(i, part):
         for k in (1, 2, 3):
-            block = chunk(wq, wo, other, pieces[k], core, part)
-            remote(block, block, spread_send.at[part, k], spread_recv.at[part, k], side_dev).wait_recv()
-            to_core(part, k)
-
-    for part in range(4):
-        await_flip(part)
-        spread(part)
-        to_core(part, 0)
-        if part > 0:
-            gather_rest(part - 1)
-    gather_rest(3)
-    for part in range(4):
-        for k in range(4):
-            block = chunk(wq, wo, other, pieces[k], 1 - core, part)
-            remote(block, block, core_send.at[part, k], core_recv.at[part, k], core_dev).wait_recv()
+            block = chunk(held, other, pieces[k], core, part)
+            remote(block, block, spread_send.at[i, k], spread_recv.at[i, k], side_dev).wait_recv()
+        go(core_copy(i, part, core))
+
+    for i, part in enumerate(PARTS):
+        spread(i, part)
+        if i > 0:
+            gather_rest(i - 1, PARTS[i - 1])
+    gather_rest(len(PARTS) - 1, PARTS[-1])
+    for i, part in enumerate(PARTS):
+        core_copy(i, part, 1 - core).wait_recv()
 
     def transpose_weights():
         def one(k, carry):
@@ -413,42 +426,44 @@
     def _():
         cot_hop.wait()
 
-    @pl.when(y < 3)
-    def _():
-        c_hop.wait_recv()
-
-    def run_backward(layer):
-        c = upstream[layer + 1]
-        d_attention = mm(c, wo[layer]).astype(BF16)
-        attention_backward(joined[layer], d_attention, probs, dj, layer)
+    def run_backward(layer, half):
+        rows = pl.ds(64 * half, 64)
+        d_attention = mm(upstream[layer + 1, rows], wo[layer]).astype(BF16)
+        attention_backward(joined[layer], d_attention, probs, dj, carried, layer, half)
 
         @pl.when((layer > 0) | (y > 0))
         def _():
-            d_normed = mm(dj[layer, 0:SEQ], wqt[layer])
-            wide = hidden[layer].astype(F32)
+            d_normed = mm(dj[layer, rows], wqt[layer])
+            wide = hidden[layer, rows].astype(F32)
             inverse = inverse_norm(wide)
             scaled = wide * inverse
             along = jnp.mean(d_normed * scaled, axis=-1, keepdims=True)
-            upstream[layer] = (
-                upstream[layer + 1].astype(F32) + inverse * (d_normed - scaled * along)
+            upstream[layer, rows] = (
+                upstream[layer + 1, rows].astype(F32) + inverse * (d_normed - scaled * along)
             ).astype(BF16)
 
-    def backward(step, carry):
-        layer = 1 - step
-
-        @pl.when(y == 0)
+    for half in (1, 0):
+        @pl.when(y < 3)
         def _():
-            send_c(layer)
-
-        run_backward(layer)
-        share(dj, layer, 2 + layer).start()
-        return carry
-
-    lax.fori_loop(0, 2, backward, 0)
-
-    @pl.when(y > 0)
-    def _():
-        c_hop.start()
+            c_hop[half].wait_recv()
+
+        def backward(step, carry):
+            layer = 1 - step
+            if half == 0:
+                @pl.when(y == 0)
+                def _():
+                    send_c(layer)
+
+            run_backward(layer, half)
+            if half == 0:
+                share(dj, layer, 2 + layer).start()
+            return carry
+
+        lax.fori_loop(0, 2, backward, 0)
+
+        @pl.when(y > 0)
+        def _():
+            c_hop[half].start()
 
     @pl.when(y == 3)
     def _():
@@ -625,7 +640,13 @@
 
     @pl.when(y > 0)
     def _():
-        c_hop.wait_send()
+        c_hop[0].wait_send()
+        c_hop[1].wait_send()
+
+
+def split_columns(total_ref, gq_ref, go_ref):
+    gq_ref[0] = total_ref[:, :QKV]
+    go_ref[0] = total_ref[:, QKV:]
 
 
 def on_device(inputs, cotangent, w_qkv, w_out):
@@ -664,6 +685,7 @@
             pltpu.VMEM((2, 8, SEQ, D), BF16),
             pltpu.VMEM((3, SEQ, D), BF16),
             pltpu.VMEM((2, 2 * SEQ, QKV), BF16),
+            pltpu.VMEM((2, 2, 2, 64, 128), F32),
             pltpu.VMEM((2, 2, 4, SEQ, 128), BF16),
             pltpu.VMEM((2, 8, SEQ, 128), BF16),
             pltpu.VMEM((4, 4, 64, QKV), BF16),
@@ -675,16 +697,16 @@
             pltpu.VMEM((64, D), BF16),
             pltpu.VMEM((64, D), BF16),
             dma((6,)),
-            dma((4,)),
-            dma((4,)),
-            dma((4, 4)),
-            dma((4, 4)),
-            dma((4, 4)),
-            dma((4, 4)),
+            dma((len(PARTS),)),
+            dma((len(PARTS),)),
+            dma((len(PARTS), 4)),
+            dma((len(PARTS), 4)),
+            dma((len(PARTS),)),
+            dma((len(PARTS),)),
             dma((2,)),
             dma((2,)),
-            dma((4,)),
-            dma((4,)),
+            dma((5,)),
+            dma((5,)),
             dma((4,)),
             dma((4,)),
             dma((2, 4)),
@@ -700,7 +722,10 @@
             collective_id=0, has_side_effects=True, vmem_limit_bytes=56 * 2**20
         ),
     )(inputs, cotangent, w_qkv, w_out)
-    return (total[None, :, :QKV], total[None, :, QKV:])
+    return pl.pallas_call(
+        split_columns,
+        out_shape=(jax.ShapeDtypeStruct((1, 64, QKV), F32), jax.ShapeDtypeStruct((1, 64, D), F32)),
+    )(total)
 
 
 def solution(mesh):

time: 134 us -> 126 us (0.940)
  Pallas kernels: 129 us -> 125 us
  local copies, waits for them, and re-layouts: 3.44 us -> 0 us
    pallas_call x1, Pallas kernels: 129 us -> 123 us  [on_device(): pl.pallas_call(kernel, out_shape=jax.ShapeDtypeStruct((64, COLS), F32), i...]
    broadcast_in_dim x2 -> x0, local copies, waits for them, and re-layouts: 3.44 us -> none  [on_device(): return (total[None, :, :QKV], total[None, :, QKV:])]
    pallas_call x0 -> x1, Pallas kernels: none -> 1.95 us  [on_device(): pl.pallas_call(split_columns, out_shape=(jax.ShapeDtypeStruct((1, 64, QKV...]
where the time goes in v4:
time: 126 us
  Pallas kernels  125 us (99%)
    pallas_call x1, Pallas kernels, on_device(): pl.pallas_call(kernel, out_shape=jax.ShapeDtypeStruct((64, COLS), F32), i...  123 us

profile of v4, /device:TPU:0, one launch (start us, length us, event | category | flops | bytes accessed | tf_op | source)
XLA Modules:
  0.0 126.0 jit_solution(1247026069741191983)
XLA Ops:
  0.6 123.4 %shard_map.59.total_ref = f32[64,2560]{1,0:T(8,128)} custom-call(bf16[1,2,1,128,1024]{4,3,2,1,0:T(8,128)(2,1)} %inputs_ref.1, bf16[1,2,1,128,1024]{4,3,2,1,0:T(8,128)(2,1)} %cotangent_ref.1, bf16[1,1024,1536]{2,1,0:T(8,128)(2,1)} %wq_ref.1, bf16[1,1024,1024]{2,1,0:T(8,128)(2,1)} %wo_ref.1), custom_call_target="tpu_custom_call" | custom-call | tf_op jit(solution)/shard_map/pallas_call | solution.py:670
  124.1 1.9 %shard_map.60 = (f32[1,64,1536]{2,1,0:T(8,128)}, f32[1,64,1024]{2,1,0:T(8,128)}) custom-call(f32[64,2560]{1,0:T(8,128)} %shard_map.59.total_ref), custom_call_target="tpu_custom_call" | custom-call | tf_op jit(solution)/shard_map/pallas_call | solution.py:725

commit v5 on v4

--- a/solution.py
+++ b/solution.py
@@ -43,13 +43,16 @@
     return jnp.concatenate([jnp.where(low, first, zero), jnp.where(low, zero, second)], axis=0).astype(BF16)
 
 
-def half_sums(x):
-    return (jnp.sum(x[:, :128], axis=1, keepdims=True), jnp.sum(x[:, 128:], axis=1, keepdims=True))
-
-
 def stack_pairs(x, group):
     at = group * 256
-    return jnp.concatenate([x[:, at : at + 128], x[:, at + 128 : at + 256]], axis=0)
+    blocks = []
+    for start in range(0, x.shape[0], 64):
+        blocks += [x[start : start + 64, at : at + 128], x[start : start + 64, at + 128 : at + 256]]
+    return jnp.concatenate(blocks, axis=0)
+
+
+def head_sums(x):
+    return (jnp.sum(x[:128], axis=0, keepdims=True), jnp.sum(x[128:], axis=0, keepdims=True))
 
 
 def kv_pairs(joined, group):
@@ -57,47 +60,47 @@
     return joined[:, D + at : D + at + 128], joined[:, D + 256 + at : D + 256 + at + 128]
 
 
-def attention_forward(joined, probs_ref, att_ref, layer):
-    rows = lax.broadcasted_iota(jnp.int32, (256, 256), 0) & 127
-    cols = lax.broadcasted_iota(jnp.int32, (256, 256), 1) & 127
-    causal = rows >= cols
+def attention_forward(joined, probs_ref, keys_ref, values_ref, att_ref, layer):
+    key = lax.broadcasted_iota(jnp.int32, (256, 256), 0) & 127
+    column = lax.broadcasted_iota(jnp.int32, (256, 256), 1)
+    causal = key <= (column & 63) + 64 * lax.shift_right_logical(column, 7)
     for group in range(4):
         queries = stack_pairs(joined, group)
-        keys, values = kv_pairs(joined, group)
-        scores = mm_nt(queries, block_diagonal(keys, group)) * 0.125
+        keys, values = (block_diagonal(pair, group) for pair in kv_pairs(joined, group))
+        keys_ref[layer, group] = keys
+        values_ref[layer, group] = values
+        scores = mm_nt(keys, queries) * 0.125
         exponent = jnp.where(causal, jnp.exp(scores), 0.0)
-        left, right = half_sums(exponent)
-        probs = jnp.concatenate([exponent[:, :128] * (1.0 / left), exponent[:, 128:] * (1.0 / right)], axis=1).astype(BF16)
+        first, second = head_sums(exponent)
+        probs = jnp.concatenate([exponent[:128] * (1.0 / first), exponent[128:] * (1.0 / second)], axis=0).astype(BF16)
         probs_ref[layer, group] = probs
-        mixed = mm(probs, block_diagonal(values, group)).astype(BF16)
+        mixed = mm_tn(probs, values).astype(BF16)
         at = group * 256
-        att_ref[:, at : at + 128] = mixed[:128]
-        att_ref[:, at + 128 : at + 256] = mixed[128:]
-
-
-def attention_backward(joined, d_attention, probs_ref, dj_ref, carried, layer, half):
-    at = 64 * half
-    rows = pl.ds(at, 64)
+        for half in range(2):
+            rows = slice(64 * half, 64 * half + 64)
+            att_ref[rows, at : at + 128] = mixed[128 * half : 128 * half + 64]
+            att_ref[rows, at + 128 : at + 256] = mixed[128 * half + 64 : 128 * half + 128]
+
+
+def attention_backward(joined, d_attention, probs_ref, keys_ref, values_ref, dj_ref, carried, layer, half):
+    rows = pl.ds(64 * half, 64)
     early, late = slice(0, 64), slice(64, 128)
     d_keys, d_values = [], []
     for group in range(4):
-        queries = stack_pairs(joined[at : at + 64], group)
+        queries = stack_pairs(joined, group)
         d_heads = stack_pairs(d_attention, group)
-        keys, values = kv_pairs(joined, group)
-        probs = jnp.concatenate(
-            [probs_ref[layer, group, at : at + 64], probs_ref[layer, group, 128 + at : 192 + at]], axis=0
-        )
-        d_probs = mm_nt(d_heads, block_diagonal(values, group))
+        probs = probs_ref[layer, group, :, 128 * half : 128 * half + 128]
+        d_probs = mm_nt(values_ref[layer, group], d_heads)
         wide = probs.astype(F32)
-        left, right = half_sums(wide * d_probs)
-        centred = jnp.concatenate([d_probs[:, :128] - left, d_probs[:, 128:] - right], axis=1)
+        first, second = head_sums(wide * d_probs)
+        centred = jnp.concatenate([d_probs[:128] - first, d_probs[128:] - second], axis=0)
         d_scores = (wide * centred * 0.125).astype(BF16)
-        d_queries = mm(d_scores, block_diagonal(keys, group)).astype(BF16)
+        d_keys.append(mm(d_scores, queries))
+        d_values.append(mm(probs, d_heads))
+        d_queries = mm_tn(d_scores, keys_ref[layer, group]).astype(BF16)
         lane = group * 256
         dj_ref[layer, rows, lane : lane + 128] = d_queries[:64]
         dj_ref[layer, rows, lane + 128 : lane + 256] = d_queries[64:]
-        d_keys.append(mm_tn(d_scores, queries))
-        d_values.append(mm_tn(probs, d_heads))
     low = lax.broadcasted_iota(jnp.int32, (128, 128), 1) < 64
 
     def merged(even, odd):
@@ -123,7 +126,7 @@
 def kernel(
     inputs_ref, cotangent_ref, wq_ref, wo_ref,
     out_ref,
-    wq, wo, wqt, entry, passed, hidden, normed, joined, probs, att, upstream, dj, carried, c_pack, c_all, grads, grads_out,
+    wq, wo, wqt, entry, passed, hidden, normed, joined, probs, keys, values, att, upstream, dj, carried, c_pack, c_all, grads, grads_out,
     z_a1, z_b1, z_m2, z_p2, z_r, z_sa1, z_sb1, z_sm2, z_sp2,
     x_a1, x_b1, x_m2, x_p2, x_r, x_sa1, x_sb1, x_sm2, x_sp2,
     o_a1, o_b1, o_m2, o_p2,
@@ -213,7 +216,7 @@
         inverse = inverse_norm(wide)
         normed[layer, 0:SEQ] = (wide * inverse).astype(BF16)
         joined[layer] = (mm(h, wq[weights]) * inverse).astype(BF16)
-        attention_forward(joined[layer], probs, att.at[layer, slot], layer)
+        attention_forward(joined[layer], probs, keys, values, att.at[layer, slot], layer)
         return (wide + mm_nt(att[layer, slot], wo[weights])).astype(BF16)
 
     across = [remote(passed.at[s], entry.at[s], entry_send.at[s], entry_recv.at[s], flip_dev) for s in range(2)]
@@ -348,38 +351,48 @@
             buf.at[layer, 0:SEQ], buf.at[layer, SEQ : 2 * SEQ], share_send.at[number], share_recv.at[number], core_dev
         )
 
-    shares = [share(normed, 0, 0), share(normed, 1, 1), share(dj, 0, 2), share(dj, 1, 3)]
+    shares = [share(dj, 0, 0), share(dj, 1, 1)]
+    share_normed = remote(
+        normed.at[:, 0:SEQ], normed.at[:, SEQ : 2 * SEQ], share_send.at[2], share_recv.at[2], core_dev
+    )
     sent.extend(shares)
 
-    def att_copy(layer, k, to_core=False):
-        if to_core:
-            block = att.at[layer, 2 * lax.rem(z + 4 - k, 4) + core]
-            return remote(block, block, att_core_send.at[layer, k], att_core_recv.at[layer, k], core_dev)
-        block = att.at[layer, slot]
-        return remote(block, block, att_send.at[layer, k], att_recv.at[layer, k], column[k][0])
-
-    spread_att = [att_copy(layer, k) for layer in (1, 0) for k in (1, 3, 2)]
-    core_att = [att_copy(layer, k, True) for layer in (1, 0) for k in (0, 1, 3, 2)]
-    sent.extend(spread_att + core_att)
+    def att_block(k, half):
+        return att.at[:, 2 * lax.rem(z + 4 - k, 4) + half]
+
+    def att_copy(k):
+        return remote(att_block(0, core), att_block(0, core), att_send.at[k], att_recv.at[k], column[k][0])
+
+    def core_att(k):
+        return remote(att_block(k, core), att_block(k, core), att_core_send.at[k], att_core_recv.at[k], core_dev)
 
     def send_attention():
-        shares[0].start()
-        shares[1].start()
-        for copy in spread_att:
-            copy.start()
+        share_normed.start()
+        for k in (1, 3, 2):
+            att_copy(k).start()
 
     def pass_attention():
-        for layer in (1, 0):
-            for k in (0, 1, 3, 2):
-                if k:
-                    block = att.at[layer, 2 * lax.rem(z + 4 - k, 4) + core]
-                    remote(block, block, att_send.at[layer, k], att_recv.at[layer, k], core_dev).wait_recv()
-                att_copy(layer, k, True).start()
-
-    def await_attention(layer):
+        core_att(0).start()
+        for k in (1, 3, 2):
+            remote(att_block(k, core), att_block(k, core), att_send.at[k], att_recv.at[k], core_dev).wait_recv()
+            core_att(k).start()
+
+    def await_attention():
         for k in range(4):
-            block = att.at[layer, 2 * lax.rem(z + 4 - k, 4) + 1 - core]
-            remote(block, block, att_core_send.at[layer, k], att_core_recv.at[layer, k], core_dev).wait_recv()
+            block = att_block(k, 1 - core)
+            remote(block, block, att_core_send.at[k], att_core_recv.at[k], core_dev).wait_recv()
+
+    early = sent[: -len(shares)]
+    del sent[: len(early)]
+
+    def settle():
+        for copy in early:
+            copy.wait_send()
+        share_normed.wait_send()
+        for k in (1, 3, 2):
+            att_copy(k).wait_send()
+        for k in range(4):
+            core_att(k).wait_send()
 
     def c_copy(layer, k, c):
         source = c_pack.at[layer, core if c == 0 else 1 - core, lax.rem(z + k, 4)]
@@ -409,14 +422,15 @@
 
     sent.extend(c_copy(layer, k, c) for layer in range(2) for k in range(4) for c in range(2) if (k, c) != (0, 0))
 
-    @pl.when(y < 3)
-    def _():
-        send_attention()
+    send_attention()
 
     @pl.when(y < 2)
     def _():
         transpose_weights()
         pass_attention()
+        await_attention()
+        share_normed.wait_recv()
+        settle()
 
     @pl.when((y == 3) & near)
     def _():
@@ -429,7 +443,7 @@
     def run_backward(layer, half):
         rows = pl.ds(64 * half, 64)
         d_attention = mm(upstream[layer + 1, rows], wo[layer]).astype(BF16)
-        attention_backward(joined[layer], d_attention, probs, dj, carried, layer, half)
+        attention_backward(joined[layer, rows], d_attention, probs, keys, values, dj, carried, layer, half)
 
         @pl.when((layer > 0) | (y > 0))
         def _():
@@ -456,7 +470,7 @@
 
             run_backward(layer, half)
             if half == 0:
-                share(dj, layer, 2 + layer).start()
+                share(dj, layer, layer).start()
             return carry
 
         lax.fori_loop(0, 2, backward, 0)
@@ -465,9 +479,14 @@
         def _():
             c_hop[half].start()
 
-    @pl.when(y == 3)
-    def _():
-        send_attention()
+    @pl.when(y > 0)
+    def _():
+        send_c(1)
+        send_c(0)
+
+    @pl.when(y >= 2)
+    def _():
+        share_normed.wait_recv()
 
     low = lax.broadcasted_iota(jnp.int32, (2 * SEQ, 128), 1) < 64
 
@@ -492,7 +511,6 @@
 
     def gradient_out(layer):
         await_c(layer)
-        await_attention(layer)
         part = mm_tn(c_all[layer].reshape(8 * SEQ, 128), att[layer].reshape(8 * SEQ, D)).astype(BF16)
         grads_out[2 * layer : 2 * layer + 2] = part.reshape(2, 64, D)
 
@@ -585,24 +603,18 @@
         z_r[pair] = (grads[pair, z, :, 0:HALF].astype(F32) + z_m2[pair].astype(F32) + z_p2[pair].astype(F32)).astype(BF16)
 
     shares[1].wait_recv()
-    shares[3].wait_recv()
     gradient(1)
     z_big[1][0]()
     x_big[0](1)
     shares[0].wait_recv()
-    shares[2].wait_recv()
     gradient(0)
     z_big[0][0]()
     x_big[0](0)
 
-    @pl.when(y > 0)
-    def _():
-        send_c(1)
-        send_c(0)
-
     @pl.when(y >= 2)
     def _():
         pass_attention()
+        await_attention()
 
     gradient_out(1)
     gradient_out(0)
@@ -631,6 +643,10 @@
     x_small[2]()
     out_ref[:, HALF:QKV] = x_r[z].astype(F32) + x_sm2[...].astype(F32) + x_sp2[...].astype(F32)
 
+    @pl.when(y >= 2)
+    def _():
+        settle()
+
     for copy in sent:
         copy.wait_send()
 
@@ -682,6 +698,8 @@
             pltpu.VMEM((2, 2 * SEQ, D), BF16),
             pltpu.VMEM((2, SEQ, QKV), BF16),
             pltpu.VMEM((2, 4, 256, 256), BF16),
+            pltpu.VMEM((2, 4, 256, 128), BF16),
+            pltpu.VMEM((2, 4, 256, 128), BF16),
             pltpu.VMEM((2, 8, SEQ, D), BF16),
             pltpu.VMEM((3, SEQ, D), BF16),
             pltpu.VMEM((2, 2 * SEQ, QKV), BF16),
@@ -709,10 +727,10 @@
             dma((5,)),
             dma((4,)),
             dma((4,)),
-            dma((2, 4)),
-            dma((2, 4)),
-            dma((2, 4)),
-            dma((2, 4)),
+            dma((4,)),
+            dma((4,)),
+            dma((4,)),
+            dma((4,)),
             dma((2, 8)),
             dma((2, 8)),
             dma((36,)),

time: 126 us -> 121 us (0.960)
  Pallas kernels: 125 us -> 120 us
    pallas_call x1, Pallas kernels: 123 us -> 118 us  [on_device(): pl.pallas_call(kernel, out_shape=jax.ShapeDtypeStruct((64, COLS), F32), i...]
where the time goes in v5:
time: 121 us
  Pallas kernels  120 us (99%)
    pallas_call x1, Pallas kernels, on_device(): pl.pallas_call(kernel, out_shape=jax.ShapeDtypeStruct((64, COLS), F32), i...  118 us

profile of v5, /device:TPU:0, one launch (start us, length us, event | category | flops | bytes accessed | tf_op | source)
XLA Modules:
  0.0 120.6 jit_solution(18152920630253057875)
XLA Ops:
  0.6 118.0 %shard_map.59.total_ref = f32[64,2560]{1,0:T(8,128)} custom-call(bf16[1,2,1,128,1024]{4,3,2,1,0:T(8,128)(2,1)} %inputs_ref.1, bf16[1,2,1,128,1024]{4,3,2,1,0:T(8,128)(2,1)} %cotangent_ref.1, bf16[1,1024,1536]{2,1,0:T(8,128)(2,1)} %wq_ref.1, bf16[1,1024,1024]{2,1,0:T(8,128)(2,1)} %wo_ref.1), custom_call_target="tpu_custom_call" | custom-call | tf_op jit(solution)/shard_map/pallas_call | solution.py:686
  118.6 1.9 %shard_map.60 = (f32[1,64,1536]{2,1,0:T(8,128)}, f32[1,64,1024]{2,1,0:T(8,128)}) custom-call(f32[64,2560]{1,0:T(8,128)} %shard_map.59.total_ref), custom_call_target="tpu_custom_call" | custom-call | tf_op jit(solution)/shard_map/pallas_call | solution.py:743

commit v6 on v5

--- a/solution.py
+++ b/solution.py
@@ -16,8 +16,9 @@
 SEQ = 128
 QKV = 1536
 COLS = 2560
-HALF = 768
-QUARTER = 384
+Z_CUT = (512, 384)
+X_CUT = (256, 384)
+HALF = sum(Z_CUT)
 WIDE = 512
 PARTS = [("q", k, 32) for k in range(4)] + [("o", k, 64) for k in range(2)]
 
@@ -83,13 +84,13 @@
 
 
 def attention_backward(joined, d_attention, probs_ref, keys_ref, values_ref, dj_ref, carried, layer, half):
-    rows = pl.ds(64 * half, 64)
-    early, late = slice(0, 64), slice(64, 128)
+    rows = pl.ds(pl.multiple_of(64 * half, 64), 64)
+    lanes = pl.ds(pl.multiple_of(128 * half, 128), 128)
     d_keys, d_values = [], []
     for group in range(4):
         queries = stack_pairs(joined, group)
         d_heads = stack_pairs(d_attention, group)
-        probs = probs_ref[layer, group, :, 128 * half : 128 * half + 128]
+        probs = probs_ref[layer, group, :, lanes]
         d_probs = mm_nt(values_ref[layer, group], d_heads)
         wide = probs.astype(F32)
         first, second = head_sums(wide * d_probs)
@@ -112,11 +113,9 @@
         for pair in range(2):
             total = merged(parts[2 * pair], parts[2 * pair + 1])
             lane = D + 256 * number + 128 * pair
-            if half:
-                carried[layer, number, pair] = total[early]
-                dj_ref[layer, rows, lane : lane + 128] = total[late].astype(BF16)
-            else:
-                dj_ref[layer, rows, lane : lane + 128] = (total[early] + carried[layer, number, pair]).astype(BF16)
+            ours = jnp.where(half == 1, total[64:], total[:64] + carried[layer, number, pair])
+            dj_ref[layer, rows, lane : lane + 128] = ours.astype(BF16)
+            carried[layer, number, pair] = total[:64]
 
 
 def inverse_norm(wide):
@@ -126,12 +125,12 @@
 def kernel(
     inputs_ref, cotangent_ref, wq_ref, wo_ref,
     out_ref,
-    wq, wo, wqt, entry, passed, hidden, normed, joined, probs, keys, values, att, upstream, dj, carried, c_pack, c_all, grads, grads_out,
+    wq, wo, wqt, wot, entry, passed, hidden, normed, joined, probs, keys, values, att, upstream, dj, carried, c_all, grads, grads_out,
     z_a1, z_b1, z_m2, z_p2, z_r, z_sa1, z_sb1, z_sm2, z_sp2,
     x_a1, x_b1, x_m2, x_p2, x_r, x_sa1, x_sb1, x_sm2, x_sp2,
     o_a1, o_b1, o_m2, o_p2,
     load_sem, flip_send, flip_recv, spread_send, spread_recv, core_send, core_recv,
-    entry_send, entry_recv, hop_send, hop_recv, share_send, share_recv,
+    entry_send, entry_recv, hop_send, hop_recv, c_hop_send, c_hop_recv, share_send, share_recv,
     att_send, att_recv, att_core_send, att_core_recv, c_send, c_recv, sum_send, sum_recv,
 ):
     section, dp = lax.axis_index("section"), lax.axis_index("dp")
@@ -203,21 +202,39 @@
         cot_hop.start()
 
     h_hop = remote(hidden.at[2], hidden.at[0], hop_send.at[0], hop_recv.at[0], yp_dev)
-    c_hop = [
-        remote(
-            upstream.at[0, 64 * half : 64 * half + 64], upstream.at[2, 64 * half : 64 * half + 64],
-            hop_send.at[(1, 4)[half]], hop_recv.at[(1, 4)[half]], ym_dev,
-        )
-        for half in range(2)
-    ]
-
-    def run_forward(h, weights, layer):
+    def run_forward(h, weights, layer, turned=False):
         wide = h.astype(F32)
         inverse = inverse_norm(wide)
         normed[layer, 0:SEQ] = (wide * inverse).astype(BF16)
         joined[layer] = (mm(h, wq[weights]) * inverse).astype(BF16)
         attention_forward(joined[layer], probs, keys, values, att.at[layer, slot], layer)
-        return (wide + mm_nt(att[layer, slot], wo[weights])).astype(BF16)
+        update = mm(att[layer, slot], wot[weights]) if turned else mm_nt(att[layer, slot], wo[weights])
+        return (wide + update).astype(BF16)
+
+    other = 1 - x_hi
+    piece = lax.rem(z + 2 * x_lo, 4)
+    pieces = [lax.rem(piece + k, 4) for k in range(4)]
+
+    def chunk(buf, slot, which, half, part):
+        name, k, rows = part
+        at = (half * 4 + which) * 128 + k * rows
+        return buf[name].at[slot, pl.ds(pl.multiple_of(at, rows), rows)]
+
+    held, given = {"q": wq, "o": wo}, {"q": wq_ref, "o": wo_ref}
+
+    def flip_copy(i, block, source=None):
+        return remote(block if source is None else source, block, flip_send.at[i], flip_recv.at[i], flip_dev)
+
+    flips = [
+        flip_copy(i, chunk(held, x_hi, pieces[2], core, part), chunk(given, 0, pieces[2], core, part))
+        for i, part in enumerate(PARTS)
+    ]
+    sent.extend(flips)
+
+    @pl.when((y == 0) & far)
+    def _():
+        for copy in flips:
+            copy.start()
 
     across = [remote(passed.at[s], entry.at[s], entry_send.at[s], entry_recv.at[s], flip_dev) for s in range(2)]
     onward = [
@@ -264,22 +281,10 @@
             for copy in onward:
                 copy.wait_send()
 
-    other = 1 - x_hi
-    piece = lax.rem(z + 2 * x_lo, 4)
-    pieces = [lax.rem(piece + k, 4) for k in range(4)]
-
-    def chunk(buf, slot, which, half, part):
-        name, k, rows = part
-        at = (half * 4 + which) * 128 + k * rows
-        return buf[name].at[slot, pl.ds(pl.multiple_of(at, rows), rows)]
-
-    held, given = {"q": wq, "o": wo}, {"q": wq_ref, "o": wo_ref}
-
-    def flip_copy(i, block, source=None):
-        return remote(block if source is None else source, block, flip_send.at[i], flip_recv.at[i], flip_dev)
-
-    for i, part in enumerate(PARTS):
-        go(flip_copy(i, chunk(held, x_hi, pieces[2], core, part), chunk(given, 0, pieces[2], core, part)))
+    @pl.when((y > 0) | near)
+    def _():
+        for copy in flips:
+            copy.start()
 
     def spread(i, part):
         flip_copy(i, chunk(held, other, pieces[0], core, part)).wait_recv()
@@ -322,6 +327,12 @@
 
     @pl.when(y >= 2)
     def _():
+        def one(k, carry):
+            layer, rows = lax.div(k, 4), pl.ds(pl.multiple_of(lax.rem(k, 4) * 256, 256), 256)
+            wot[layer, :, rows] = wo[layer, rows].T
+            return carry
+
+        lax.fori_loop(0, 8, one, 0)
         transpose_weights()
 
     @pl.when((y == 0) & near)
@@ -336,11 +347,17 @@
     def _():
         h_hop.wait_recv()
 
-    def forward(layer, carry):
-        hidden[layer + 1] = run_forward(hidden[layer], layer, layer)
+    def forward(turned, layer, carry):
+        hidden[layer + 1] = run_forward(hidden[layer], layer, layer, turned)
         return carry
 
-    lax.fori_loop(0, 2, forward, 0)
+    @pl.when(y < 2)
+    def _():
+        lax.fori_loop(0, 2, functools.partial(forward, False), 0)
+
+    @pl.when(y >= 2)
+    def _():
+        lax.fori_loop(0, 2, functools.partial(forward, True), 0)
 
     @pl.when((y > 0) & (y < 3))
     def _():
@@ -394,33 +411,29 @@
         for k in range(4):
             core_att(k).wait_send()
 
-    def c_copy(layer, k, c):
-        source = c_pack.at[layer, core if c == 0 else 1 - core, lax.rem(z + k, 4)]
-        return remote(source, c_all.at[layer, slot], c_send.at[layer, 2 * k + c], c_recv.at[layer, 2 * k + c], column[k][c])
+    def c_columns(layer, k):
+        return upstream.at[layer + 1, :, pl.ds(pl.multiple_of(256 * lax.rem(z + k, 4), 256), 256)]
+
+    def c_copy(layer, k):
+        return remote(c_columns(layer, k), c_all.at[layer, z, core], c_send.at[layer, k], c_recv.at[layer, k], column[k][0])
+
+    def core_c(layer, half):
+        block = c_all.at[layer, :, half]
+        return remote(block, block, c_send.at[layer, 0], c_recv.at[layer, 0], core_dev)
 
     def send_c(layer):
-        low = lax.broadcasted_iota(jnp.int32, (SEQ, 128), 1) < 64
-        for to in range(4):
-            a = upstream[layer + 1, :, 256 * to : 256 * to + 128].astype(F32)
-            b = upstream[layer + 1, :, 256 * to + 128 : 256 * to + 256].astype(F32)
-            c_pack[layer, 0, to] = jnp.where(low, a, pltpu.roll(b, 64, 1)).astype(BF16)
-            c_pack[layer, 1, to] = jnp.where(low, pltpu.roll(a, 64, 1), b).astype(BF16)
-        c_all[layer, slot] = c_pack[layer, core, z]
-        for k in (1, 3, 2, 0):
-            for c in range(2):
-                if (k, c) != (0, 0):
-                    c_copy(layer, k, c).start()
-
-    def await_c(layer):
-        for k in range(4):
-            for c in range(2):
-                if (k, c) != (0, 0):
-                    block = c_all.at[layer, 2 * lax.rem(z + 4 - k, 4) + (core if c == 0 else 1 - core)]
-                    remote(
-                        block, block, c_send.at[layer, 2 * k + c], c_recv.at[layer, 2 * k + c], core_dev
-                    ).wait_recv()
-
-    sent.extend(c_copy(layer, k, c) for layer in range(2) for k in range(4) for c in range(2) if (k, c) != (0, 0))
+        for k in (1, 3, 2):
+            c_copy(layer, k).start()
+
+    def pass_c(layer):
+        c_all[layer, z, core] = c_columns(layer, 0)[...]
+        for k in (1, 3, 2):
+            block = c_all.at[layer, lax.rem(z + 4 - k, 4), core]
+            remote(block, block, c_send.at[layer, k], c_recv.at[layer, k], core_dev).wait_recv()
+        core_c(layer, core).start()
+
+    sent.extend(c_copy(layer, k) for layer in range(2) for k in (1, 3, 2))
+    sent.extend(core_c(layer, core) for layer in range(2))
 
     send_attention()
 
@@ -440,10 +453,28 @@
     def _():
         cot_hop.wait()
 
-    def run_backward(layer, half):
-        rows = pl.ds(64 * half, 64)
+    def c_half(half):
+        rows = pl.ds(pl.multiple_of(64 * half, 64), 64)
+        return remote(upstream.at[0, rows], upstream.at[2, rows], c_hop_send.at[half], c_hop_recv.at[half], ym_dev)
+
+    def backward(step, carry):
+        half, layer = 1 - lax.div(step, 2), 1 - lax.rem(step, 2)
+        rows = pl.ds(pl.multiple_of(64 * half, 64), 64)
+
+        @pl.when((y < 3) & (layer == 1))
+        def _():
+            c_half(half).wait_recv()
+
+        @pl.when((y == 0) & (half == 0))
+        def _():
+            send_c(layer)
+
         d_attention = mm(upstream[layer + 1, rows], wo[layer]).astype(BF16)
         attention_backward(joined[layer, rows], d_attention, probs, keys, values, dj, carried, layer, half)
+
+        @pl.when(half == 0)
+        def _():
+            share(dj, layer, layer).start()
 
         @pl.when((layer > 0) | (y > 0))
         def _():
@@ -456,28 +487,13 @@
                 upstream[layer + 1, rows].astype(F32) + inverse * (d_normed - scaled * along)
             ).astype(BF16)
 
-    for half in (1, 0):
-        @pl.when(y < 3)
+        @pl.when((y > 0) & (layer == 0))
         def _():
-            c_hop[half].wait_recv()
-
-        def backward(step, carry):
-            layer = 1 - step
-            if half == 0:
-                @pl.when(y == 0)
-                def _():
-                    send_c(layer)
-
-            run_backward(layer, half)
-            if half == 0:
-                share(dj, layer, layer).start()
-            return carry
-
-        lax.fori_loop(0, 2, backward, 0)
-
-        @pl.when(y > 0)
-        def _():
-            c_hop[half].start()
+            c_half(half).start()
+
+        return carry
+
+    lax.fori_loop(0, 4, backward, 0)
 
     @pl.when(y > 0)
     def _():
@@ -510,8 +526,13 @@
             grads[2 * layer + lo] = part.reshape(4, 64, QKV)
 
     def gradient_out(layer):
-        await_c(layer)
-        part = mm_tn(c_all[layer].reshape(8 * SEQ, 128), att[layer].reshape(8 * SEQ, D)).astype(BF16)
+        core_c(layer, 1 - core).wait_recv()
+        a = c_all[layer, :, :, :, 0:128].reshape(8 * SEQ, 128).astype(F32)
+        b = c_all[layer, :, :, :, 128:256].reshape(8 * SEQ, 128).astype(F32)
+        first = jnp.where(core == 0, a, pltpu.roll(a, 64, 1))
+        second = jnp.where(core == 0, pltpu.roll(b, 64, 1), b)
+        left = jnp.where(lax.broadcasted_iota(jnp.int32, a.shape, 1) < 64, first, second).astype(BF16)
+        part = mm_tn(left, att[layer].reshape(8 * SEQ, D)).astype(BF16)
         grads_out[2 * layer : 2 * layer + 2] = part.reshape(2, 64, D)
 
     def ring_sum(view, position, plus, minus, bufs, sems, layers=None):
@@ -568,16 +589,20 @@
 
         return first, second, last
 
-    def halves(offset):
-        return [pl.ds(offset, QUARTER), pl.ds(offset + QUARTER, QUARTER)]
-
-    z_cols, x_cols, own_cols = halves(0), halves(HALF), halves(0)
-    wide_at = [(slice(None), slice(None), cols) for cols in own_cols]
-    flat_at = [(slice(None), cols) for cols in own_cols]
+    def cut(offset, widths):
+        return [pl.ds(offset, widths[0]), pl.ds(offset + widths[0], widths[1])]
+
+    z_cols, x_cols, z_own, x_own = cut(0, Z_CUT), cut(HALF, X_CUT), cut(0, Z_CUT), cut(0, X_CUT)
+
+    def wide_at(own):
+        return [(slice(None), slice(None), cols) for cols in own]
+
+    def flat_at(own):
+        return [(slice(None), cols) for cols in own]
 
     def z_ring(layer):
         pair = pl.ds(2 * layer, 2)
-        bufs = (z_a1.at[pair], z_b1.at[pair], z_m2.at[pair], z_p2.at[pair], *wide_at)
+        bufs = (z_a1.at[pair], z_b1.at[pair], z_m2.at[pair], z_p2.at[pair], *wide_at(z_own))
         return ring_sum(lambda t, k: grads.at[pair, t, :, z_cols[k]], z, zp_dev, zm_dev, bufs, 24 if layer else 0)
 
     z_big = [z_ring(0), z_ring(1)]
@@ -585,13 +610,13 @@
         return lax.div(target, 2)
 
     x_big = ring_sum(
-        lambda t, k: grads.at[t, :, :, x_cols[k]], x, xp_dev, xm_dev, (x_a1, x_b1, x_m2, x_p2, *wide_at), 6, layer_of
+        lambda t, k: grads.at[t, :, :, x_cols[k]], x, xp_dev, xm_dev, (x_a1, x_b1, x_m2, x_p2, *wide_at(x_own)), 6, layer_of
     )
     z_small = ring_sum(
-        lambda t, k: z_r.at[t, :, own_cols[k]], x, xp_dev, xm_dev, (z_sa1, z_sb1, z_sm2, z_sp2, *flat_at), 12, layer_of
+        lambda t, k: z_r.at[t, :, z_own[k]], x, xp_dev, xm_dev, (z_sa1, z_sb1, z_sm2, z_sp2, *flat_at(z_own)), 12, layer_of
     )
     x_small = ring_sum(
-        lambda t, k: x_r.at[t, :, own_cols[k]], z, zp_dev, zm_dev, (x_sa1, x_sb1, x_sm2, x_sp2, *flat_at), 18
+        lambda t, k: x_r.at[t, :, x_own[k]], z, zp_dev, zm_dev, (x_sa1, x_sb1, x_sm2, x_sp2, *flat_at(x_own)), 18
     )
     out_at = [(slice(None), pl.ds(0, WIDE)), (slice(None), pl.ds(WIDE, WIDE))]
     o_ring = ring_sum(
@@ -616,6 +641,8 @@
         pass_attention()
         await_attention()
 
+    pass_c(1)
+    pass_c(0)
     gradient_out(1)
     gradient_out(0)
     o_ring[0]()
@@ -656,8 +683,8 @@
 
     @pl.when(y > 0)
     def _():
-        c_hop[0].wait_send()
-        c_hop[1].wait_send()
+        c_half(0).wait_send()
+        c_half(1).wait_send()
 
 
 def split_columns(total_ref, gq_ref, go_ref):
@@ -670,17 +697,19 @@
     vmem = pl.BlockSpec(memory_space=pltpu.VMEM)
     dma = pltpu.SemaphoreType.DMA
 
-    def flow():
+    def flow(widths):
+        first, second = widths
+        both = first + second
         return [
-            pltpu.VMEM((4, 64, QUARTER), BF16),
-            pltpu.VMEM((4, 64, QUARTER), BF16),
-            pltpu.VMEM((4, 64, HALF), BF16),
-            pltpu.VMEM((4, 64, HALF), BF16),
-            pltpu.VMEM((4, 64, HALF), BF16),
-            pltpu.VMEM((64, QUARTER), BF16),
-            pltpu.VMEM((64, QUARTER), BF16),
-            pltpu.VMEM((64, HALF), BF16),
-            pltpu.VMEM((64, HALF), BF16),
+            pltpu.VMEM((4, 64, first), BF16),
+            pltpu.VMEM((4, 64, second), BF16),
+            pltpu.VMEM((4, 64, both), BF16),
+            pltpu.VMEM((4, 64, both), BF16),
+            pltpu.VMEM((4, 64, both), BF16),
+            pltpu.VMEM((64, first), BF16),
+            pltpu.VMEM((64, second), BF16),
+            pltpu.VMEM((64, both), BF16),
+            pltpu.VMEM((64, both), BF16),
         ]
 
     total = pl.pallas_call(
@@ -692,6 +721,7 @@
             pltpu.VMEM((2, D, QKV), BF16),
             pltpu.VMEM((2, D, D), BF16),
             pltpu.VMEM((2, QKV, D), BF16),
+            pltpu.VMEM((2, D, D), BF16),
             pltpu.VMEM((2, SEQ, D), BF16),
             pltpu.VMEM((2, SEQ, D), BF16),
             pltpu.VMEM((3, SEQ, D), BF16),
@@ -704,12 +734,11 @@
             pltpu.VMEM((3, SEQ, D), BF16),
             pltpu.VMEM((2, 2 * SEQ, QKV), BF16),
             pltpu.VMEM((2, 2, 2, 64, 128), F32),
-            pltpu.VMEM((2, 2, 4, SEQ, 128), BF16),
-            pltpu.VMEM((2, 8, SEQ, 128), BF16),
+            pltpu.VMEM((2, 4, 2, SEQ, 256), BF16),
             pltpu.VMEM((4, 4, 64, QKV), BF16),
             pltpu.VMEM((4, 64, D), BF16),
-            *flow(),
-            *flow(),
+            *flow(Z_CUT),
+            *flow(X_CUT),
             pltpu.VMEM((64, WIDE), BF16),
             pltpu.VMEM((64, WIDE), BF16),
             pltpu.VMEM((64, D), BF16),
@@ -723,16 +752,18 @@
             dma((len(PARTS),)),
             dma((2,)),
             dma((2,)),
-            dma((5,)),
-            dma((5,)),
+            dma((4,)),
+            dma((4,)),
+            dma((2,)),
+            dma((2,)),
             dma((4,)),
             dma((4,)),
             dma((4,)),
             dma((4,)),
             dma((4,)),
             dma((4,)),
-            dma((2, 8)),
-            dma((2, 8)),
+            dma((2, 4)),
+            dma((2, 4)),
             dma((36,)),
             dma((36,)),
         ],

time: 121 us -> 118 us (0.975)
  Pallas kernels: 120 us -> 117 us
    pallas_call x1, Pallas kernels: 118 us -> 115 us  [on_device(): pl.pallas_call(kernel, out_shape=jax.ShapeDtypeStruct((64, COLS), F32), i...]
where the time goes in v6:
time: 118 us
  Pallas kernels  117 us (99%)
    pallas_call x1, Pallas kernels, on_device(): pl.pallas_call(kernel, out_shape=jax.ShapeDtypeStruct((64, COLS), F32), i...  115 us

profile of v6, /device:TPU:0, one launch (start us, length us, event | category | flops | bytes accessed | tf_op | source)
XLA Modules:
  0.0 118.0 jit_solution(2545654100708910163)
XLA Ops:
  0.6 115.4 %shard_map.59.total_ref = f32[64,2560]{1,0:T(8,128)} custom-call(bf16[1,2,1,128,1024]{4,3,2,1,0:T(8,128)(2,1)} %inputs_ref.1, bf16[1,2,1,128,1024]{4,3,2,1,0:T(8,128)(2,1)} %cotangent_ref.1, bf16[1,1024,1536]{2,1,0:T(8,128)(2,1)} %wq_ref.1, bf16[1,1024,1024]{2,1,0:T(8,128)(2,1)} %wo_ref.1), custom_call_target="tpu_custom_call" | custom-call | tf_op jit(solution)/shard_map/pallas_call | solution.py:715
  116.0 1.9 %shard_map.60 = (f32[1,64,1536]{2,1,0:T(8,128)}, f32[1,64,1024]{2,1,0:T(8,128)}) custom-call(f32[64,2560]{1,0:T(8,128)} %shard_map.59.total_ref), custom_call_target="tpu_custom_call" | custom-call | tf_op jit(solution)/shard_map/pallas_call | solution.py:774

commit v7 on v6

--- a/solution.py
+++ b/solution.py
@@ -185,10 +185,9 @@
         load_cot.start()
 
     barrier = pltpu.get_barrier_semaphore()
-    ring = [column[k][c] for k in range(4) for c in range(2) if (k, c) != (0, 0)]
-    for device in (*ring, xp_dev, xm_dev, yp_dev, ym_dev, up_across_dev, down_across_dev):
+    for device in (core_dev, xp_dev, xm_dev, zp_dev, zm_dev, yp_dev, ym_dev):
         pl.semaphore_signal(barrier, inc=1, device_id=device, device_id_type=MESH)
-    pl.semaphore_wait(barrier, 13)
+    pl.semaphore_wait(barrier, 7)
 
     in_hop = remote(inputs_ref.at[0, 1, 0], hidden.at[0], hop_send.at[2], hop_recv.at[2], side_dev)
     cot_hop = remote(cotangent_ref.at[0, 1, 0], upstream.at[2], hop_send.at[3], hop_recv.at[3], side_dev)

time: 118 us -> 117 us (level)
    pallas_call x1, Pallas kernels: 115 us -> 114 us  [on_device(): pl.pallas_call(kernel, out_shape=jax.ShapeDtypeStruct((64, COLS), F32), i...]
where the time goes in v7:
time: 117 us; the launch traced here: 116 us
  Pallas kernels  116 us (99%)
    pallas_call x1, Pallas kernels, on_device(): pl.pallas_call(kernel, out_shape=jax.ShapeDtypeStruct((64, COLS), F32), i...  114 us

profile of v7, /device:TPU:0, one launch (start us, length us, event | category | flops | bytes accessed | tf_op | source)
XLA Modules:
  0.0 116.5 jit_solution(13239938102132936315)
XLA Ops:
  0.6 113.9 %shard_map.59.total_ref = f32[64,2560]{1,0:T(8,128)} custom-call(bf16[1,2,1,128,1024]{4,3,2,1,0:T(8,128)(2,1)} %inputs_ref.1, bf16[1,2,1,128,1024]{4,3,2,1,0:T(8,128)(2,1)} %cotangent_ref.1, bf16[1,1024,1536]{2,1,0:T(8,128)(2,1)} %wq_ref.1, bf16[1,1024,1024]{2,1,0:T(8,128)(2,1)} %wo_ref.1), custom_call_target="tpu_custom_call" | custom-call | tf_op jit(solution)/shard_map/pallas_call | solution.py:714
  114.5 1.9 %shard_map.60 = (f32[1,64,1536]{2,1,0:T(8,128)}, f32[1,64,1024]{2,1,0:T(8,128)}) custom-call(f32[64,2560]{1,0:T(8,128)} %shard_map.59.total_ref), custom_call_target="tpu_custom_call" | custom-call | tf_op jit(solution)/shard_map/pallas_call | solution.py:773

commit v8 on v7

--- a/solution.py
+++ b/solution.py
@@ -201,14 +201,20 @@
         cot_hop.start()
 
     h_hop = remote(hidden.at[2], hidden.at[0], hop_send.at[0], hop_recv.at[0], yp_dev)
-    def run_forward(h, weights, layer, turned=False):
+    def attend(h, weights, layer):
         wide = h.astype(F32)
         inverse = inverse_norm(wide)
         normed[layer, 0:SEQ] = (wide * inverse).astype(BF16)
         joined[layer] = (mm(h, wq[weights]) * inverse).astype(BF16)
         attention_forward(joined[layer], probs, keys, values, att.at[layer, slot], layer)
+
+    def project(h, weights, layer, turned):
         update = mm(att[layer, slot], wot[weights]) if turned else mm_nt(att[layer, slot], wo[weights])
-        return (wide + update).astype(BF16)
+        return (h.astype(F32) + update).astype(BF16)
+
+    def run_forward(h, weights, layer, turned=False):
+        attend(h, weights, layer)
+        return project(h, weights, layer, turned)
 
     other = 1 - x_hi
     piece = lax.rem(z + 2 * x_lo, 4)
@@ -303,13 +309,30 @@
             remote(block, block, spread_send.at[i, k], spread_recv.at[i, k], side_dev).wait_recv()
         go(core_copy(i, part, core))
 
+    def await_core(name):
+        for i, part in enumerate(PARTS):
+            if part[0] == name:
+                core_copy(i, part, 1 - core).wait_recv()
+
+    @pl.when(y > 0)
+    def _():
+        for copy in loads:
+            copy.wait()
+
     for i, part in enumerate(PARTS):
         spread(i, part)
         if i > 0:
             gather_rest(i - 1, PARTS[i - 1])
+
     gather_rest(len(PARTS) - 1, PARTS[-1])
-    for i, part in enumerate(PARTS):
-        core_copy(i, part, 1 - core).wait_recv()
+    await_core("q")
+
+    @pl.when(y == 1)
+    def _():
+        h_hop.wait_recv()
+        attend(hidden[0], 0, 0)
+
+    await_core("o")
 
     def transpose_weights():
         def one(k, carry):
@@ -319,11 +342,6 @@
 
         lax.fori_loop(0, 12, one, 0)
 
-    @pl.when(y > 0)
-    def _():
-        for copy in loads:
-            copy.wait()
-
     @pl.when(y >= 2)
     def _():
         def one(k, carry):
@@ -342,12 +360,16 @@
     def _():
         in_hop.wait()
 
-    @pl.when(y > 0)
+    @pl.when(y >= 2)
     def _():
         h_hop.wait_recv()
 
     def forward(turned, layer, carry):
-        hidden[layer + 1] = run_forward(hidden[layer], layer, layer, turned)
+        if turned:
+            attend(hidden[layer], layer, layer)
+        else:
+            pl.when((y == 0) | (layer > 0))(lambda: attend(hidden[layer], layer, layer))
+        hidden[layer + 1] = project(hidden[layer], layer, layer, turned)
         return carry
 
     @pl.when(y < 2)
@@ -644,9 +666,9 @@
     pass_c(0)
     gradient_out(1)
     gradient_out(0)
-    o_ring[0]()
     z_big[1][1]()
     x_big[1](1)
+    o_ring[0]()
     z_big[0][1]()
     x_big[1](0)
     z_big[1][2]()
@@ -662,6 +684,23 @@
     z_small[1](1)
     z_small[1](0)
     x_small[1]()
+    last_sent = sent[-18:-6]
+    for copy in sent[:-18] + sent[-6:]:
+        copy.wait_send()
+
+    @pl.when(y >= 2)
+    def _():
+        settle()
+
+    @pl.when((y > 0) & (y < 3))
+    def _():
+        h_hop.wait_send()
+
+    @pl.when(y > 0)
+    def _():
+        c_half(0).wait_send()
+        c_half(1).wait_send()
+
     o_ring[2]()
     out_ref[:, QKV:COLS] = grads_out[x].astype(F32) + o_m2[...].astype(F32) + o_p2[...].astype(F32)
     z_small[2]()
@@ -669,21 +708,8 @@
     x_small[2]()
     out_ref[:, HALF:QKV] = x_r[z].astype(F32) + x_sm2[...].astype(F32) + x_sp2[...].astype(F32)
 
-    @pl.when(y >= 2)
-    def _():
-        settle()
-
-    for copy in sent:
+    for copy in last_sent:
         copy.wait_send()
-
-    @pl.when((y > 0) & (y < 3))
-    def _():
-        h_hop.wait_send()
-
-    @pl.when(y > 0)
-    def _():
-        c_half(0).wait_send()
-        c_half(1).wait_send()
 
 
 def split_columns(total_ref, gq_ref, go_ref):

time: 117 us -> 117 us (level)
  no operation moved by 1% of the time
where the time goes in v8:
time: 117 us
  Pallas kernels  116 us (99%)
    pallas_call x1, Pallas kernels, on_device(): pl.pallas_call(kernel, out_shape=jax.ShapeDtypeStruct((64, COLS), F32), i...  114 us

profile of v8, /device:TPU:0, one launch (start us, length us, event | category | flops | bytes accessed | tf_op | source)
XLA Modules:
  0.0 116.8 jit_solution(2634233814212361247)
XLA Ops:
  0.6 114.2 %shard_map.59.total_ref = f32[64,2560]{1,0:T(8,128)} custom-call(bf16[1,2,1,128,1024]{4,3,2,1,0:T(8,128)(2,1)} %inputs_ref.1, bf16[1,2,1,128,1024]{4,3,2,1,0:T(8,128)(2,1)} %cotangent_ref.1, bf16[1,1024,1536]{2,1,0:T(8,128)(2,1)} %wq_ref.1, bf16[1,1024,1024]{2,1,0:T(8,128)(2,1)} %wo_ref.1), custom_call_target="tpu_custom_call" | custom-call | tf_op jit(solution)/shard_map/pallas_call | solution.py:740
  114.8 1.9 %shard_map.60 = (f32[1,64,1536]{2,1,0:T(8,128)}, f32[1,64,1024]{2,1,0:T(8,128)}) custom-call(f32[64,2560]{1,0:T(8,128)} %shard_map.59.total_ref), custom_call_target="tpu_custom_call" | custom-call | tf_op jit(solution)/shard_map/pallas_call | solution.py:799

commit v9 on v7

--- a/solution.py
+++ b/solution.py
@@ -125,7 +125,7 @@
 def kernel(
     inputs_ref, cotangent_ref, wq_ref, wo_ref,
     out_ref,
-    wq, wo, wqt, wot, entry, passed, hidden, normed, joined, probs, keys, values, att, upstream, dj, carried, c_all, grads, grads_out,
+    wq, wo, wqt, wot, entry, passed, hidden, normed, normed_t, joined, probs, keys, values, att, upstream, dj, carried, c_all, grads, grads_out,
     z_a1, z_b1, z_m2, z_p2, z_r, z_sa1, z_sb1, z_sm2, z_sp2,
     x_a1, x_b1, x_m2, x_p2, x_r, x_sa1, x_sb1, x_sm2, x_sp2,
     o_a1, o_b1, o_m2, o_p2,
@@ -434,6 +434,25 @@
     sent.extend(c_copy(layer, k) for layer in range(2) for k in (1, 3, 2))
     sent.extend(core_c(layer, core) for layer in range(2))
 
+    low = lax.broadcasted_iota(jnp.int32, (2 * SEQ, 128), 1) < 64
+
+    def own_columns(block):
+        def tile(k):
+            return block[:, 128 * k : 128 * k + 128].astype(F32)
+
+        tiles = []
+        for lo in range(2):
+            for pair in range(2):
+                a, b = tile(4 * pair + lo), tile(4 * pair + 2 + lo)
+                first = jnp.where(core == 0, a, pltpu.roll(a, 64, 1))
+                second = jnp.where(core == 0, pltpu.roll(b, 64, 1), b)
+                tiles.append(jnp.where(low, first, second).astype(BF16))
+        return jnp.concatenate(tiles, axis=1)
+
+    def turn_normed():
+        for layer in range(2):
+            normed_t[layer] = own_columns(normed[layer]).T
+
     send_attention()
 
     @pl.when(y < 2)
@@ -442,6 +461,7 @@
         pass_attention()
         await_attention()
         share_normed.wait_recv()
+        turn_normed()
         settle()
 
     @pl.when((y == 3) & near)
@@ -502,26 +522,11 @@
     @pl.when(y >= 2)
     def _():
         share_normed.wait_recv()
-
-    low = lax.broadcasted_iota(jnp.int32, (2 * SEQ, 128), 1) < 64
-
-    def own_columns(block):
-        def tile(k):
-            return block[:, 128 * k : 128 * k + 128].astype(F32)
-
-        tiles = []
+        turn_normed()
+
+    def gradient(layer):
         for lo in range(2):
-            for pair in range(2):
-                a, b = tile(4 * pair + lo), tile(4 * pair + 2 + lo)
-                first = jnp.where(core == 0, a, pltpu.roll(a, 64, 1))
-                second = jnp.where(core == 0, pltpu.roll(b, 64, 1), b)
-                tiles.append(jnp.where(low, first, second).astype(BF16))
-        return jnp.concatenate(tiles, axis=1)
-
-    def gradient(layer):
-        left = own_columns(normed[layer])
-        for lo in range(2):
-            part = mm_tn(left[:, 256 * lo : 256 * lo + 256], dj[layer]).astype(BF16)
+            part = mm(normed_t[layer, 256 * lo : 256 * lo + 256], dj[layer]).astype(BF16)
             grads[2 * layer + lo] = part.reshape(4, 64, QKV)
 
     def gradient_out(layer):
@@ -725,6 +730,7 @@
             pltpu.VMEM((2, SEQ, D), BF16),
             pltpu.VMEM((3, SEQ, D), BF16),
             pltpu.VMEM((2, 2 * SEQ, D), BF16),
+            pltpu.VMEM((2, 512, 2 * SEQ), BF16),
             pltpu.VMEM((2, SEQ, QKV), BF16),
             pltpu.VMEM((2, 4, 256, 256), BF16),
             pltpu.VMEM((2, 4, 256, 128), BF16),

time: 117 us -> 117 us (level)
  no operation moved by 1% of the time
where the time goes in v9:
time: 117 us
  Pallas kernels  116 us (99%)
    pallas_call x1, Pallas kernels, on_device(): pl.pallas_call(kernel, out_shape=jax.ShapeDtypeStruct((64, COLS), F32), i...  114 us

profile of v9, /device:TPU:0, one launch (start us, length us, event | category | flops | bytes accessed | tf_op | source)
XLA Modules:
  0.0 116.5 jit_solution(15338338568317900304)
XLA Ops:
  0.6 113.9 %shard_map.59.total_ref = f32[64,2560]{1,0:T(8,128)} custom-call(bf16[1,2,1,128,1024]{4,3,2,1,0:T(8,128)(2,1)} %inputs_ref.1, bf16[1,2,1,128,1024]{4,3,2,1,0:T(8,128)(2,1)} %cotangent_ref.1, bf16[1,1024,1536]{2,1,0:T(8,128)(2,1)} %wq_ref.1, bf16[1,1024,1024]{2,1,0:T(8,128)(2,1)} %wo_ref.1), custom_call_target="tpu_custom_call" | custom-call | tf_op jit(solution)/shard_map/pallas_call | solution.py:719
  114.6 1.9 %shard_map.60 = (f32[1,64,1536]{2,1,0:T(8,128)}, f32[1,64,1024]{2,1,0:T(8,128)}) custom-call(f32[64,2560]{1,0:T(8,128)} %shard_map.59.total_ref), custom_call_target="tpu_custom_call" | custom-call | tf_op jit(solution)/shard_map/pallas_call | solution.py:779
